TPU v7x, 128 devices: a whole 4x4x4 slice. The times are simulated.
128 devices in a mesh: row: 4 (over z_hi, core), col: 32 (over y, x, z_lo).
Axes of the slice: x: 4, y: 4, z: 4 (z_hi: 2, z_lo: 2; z = z_hi * 2 + z_lo), core: 2. Of those that a mesh axis runs over, the one named last changes fastest.
Arguments:
- field: bfloat16 [128, 2048, 512], P('row', 'col'), may hold values from -6 to 6
- w_expand: bfloat16 [512, 2048], replicated, may hold values from -0.25 to 0.25
- dw_kernel: float32 [3, 3, 2048], replicated, may hold values from -2 to 2
- w_project: bfloat16 [2048, 512], replicated, may hold values from -0.125 to 0.125
- qkv_block: bfloat16 [512, 1536], replicated, may hold values from -5 to 5
- out_block: bfloat16 [512, 512], replicated, may hold values from -0.25 to 0.25
- qkv_grid: bfloat16 [512, 1536], replicated, may hold values from -5 to 5
- out_grid: bfloat16 [512, 512], replicated, may hold values from -0.25 to 0.25
Outputs:
- result: bfloat16 [128, 2048, 512], P('row', 'col')
All inputs are finite; a program needn't handle non-finite values.
Results may differ from a plain program's by a relative error of at most 0.011.
Values may be sent and summed in bfloat16 or wider, within the bound.
No kernel may reach another device: no remote copies, remote signals or barrier semaphores. Data moves between devices by JAX's collectives and lax.ppermute only.
A program may use at most 128 MiB of HBM per device.

v0:
```python
import jax
import jax.numpy as jnp
from jax import lax
from jax.sharding import PartitionSpec as P

HEADS = 16


def extended(cells, sides, width):
    for axis, dim in sides:
        count = lax.axis_size(axis)
        ends = count - 1
        head = lax.slice_in_dim(cells, 0, width, axis=dim)
        tail = lax.slice_in_dim(cells, cells.shape[dim] - width, cells.shape[dim], axis=dim)
        cells = jnp.concatenate(
            [
                lax.ppermute(tail, axis, [(i, (i + 1) % count) for i in range(ends)]),
                cells,
                lax.ppermute(head, axis, [((i + 1) % count, i) for i in range(ends)]),
            ],
            axis=dim,
        )
    return cells


def layer_norm(v):
    mean = jnp.mean(v, axis=-1, keepdims=True)
    cent = v - mean
    var = jnp.mean(cent * cent, axis=-1, keepdims=True)
    return cent * lax.rsqrt(var + 1e-05)


def expand(rows, w_expand):
    normed = layer_norm(rows.astype(jnp.float32)).astype(jnp.bfloat16)
    pre = jnp.einsum("rwc,cd->rwd", normed, w_expand, preferred_element_type=jnp.float32)
    return jax.nn.gelu(pre, approximate=False).astype(jnp.bfloat16)


def attend(tokens, qkv, out_proj):
    groups, count, width = tokens.shape
    head_dim = width // HEADS
    normed = layer_norm(tokens.astype(jnp.float32)).astype(jnp.bfloat16)
    proj = jnp.einsum("gtc,cd->gtd", normed, qkv, preferred_element_type=jnp.float32).astype(
        jnp.bfloat16
    )
    query = proj[:, :, :width].reshape(groups, count, HEADS, head_dim)
    keys = proj[:, :, width : 2 * width].reshape(groups, count, HEADS, head_dim)
    values = proj[:, :, 2 * width :].reshape(groups, count, HEADS, head_dim)
    scores = jnp.einsum(
        "gqhd,gkhd->ghqk", query, keys, preferred_element_type=jnp.float32
    ) * head_dim ** (-0.5)
    scores = scores - jnp.max(scores, axis=-1, keepdims=True)
    weights = jnp.exp(scores)
    weights = (weights / jnp.sum(weights, axis=-1, keepdims=True)).astype(jnp.bfloat16)
    context = jnp.einsum(
        "ghqk,gkhd->gqhd", weights, values, preferred_element_type=jnp.float32
    ).astype(jnp.bfloat16)
    context = context.reshape(groups, count, width)
    update = jnp.einsum("gtc,cd->gtd", context, out_proj, preferred_element_type=jnp.float32)
    return (tokens.astype(jnp.float32) + update).astype(jnp.bfloat16)


def on_device(field, w_expand, dw_kernel, w_project, qkv_block, out_block, qkv_grid, out_grid):
    tile_h, tile_w, chans = field.shape
    hidden = expand(field, w_expand)
    padded = extended(hidden, (("row", 0), ("col", 1)), 1)
    acc = jnp.zeros((tile_h, tile_w, padded.shape[2]), jnp.float32)
    for da in range(3):
        for db in range(3):
            acc = (
                acc
                + padded[da : da + tile_h, db : db + tile_w].astype(jnp.float32) * dw_kernel[da, db]
            )
    spatial = jax.nn.gelu(acc, approximate=False).astype(jnp.bfloat16)
    proj = jnp.einsum("rwd,dc->rwc", spatial, w_project, preferred_element_type=jnp.float32)
    mixed = (field.astype(jnp.float32) + proj).astype(jnp.bfloat16)
    blocks = mixed.reshape(tile_h // 8, 8, tile_w // 8, 8, chans).transpose(0, 2, 1, 3, 4)
    blocks = attend(blocks.reshape(-1, 64, chans), qkv_block, out_block)
    blocked = (
        blocks.reshape(tile_h // 8, tile_w // 8, 8, 8, chans)
        .transpose(0, 2, 1, 3, 4)
        .reshape(tile_h, tile_w, chans)
    )
    n_row = lax.axis_size("row")
    n_col = lax.axis_size("col")
    per_tile = 8 // n_row
    sub_rows = tile_h // 8
    col_tiles = n_col // 8
    sub_cols = tile_w // n_col
    n_groups = col_tiles * sub_rows * sub_cols
    outgoing = blocked.reshape(per_tile, n_row, sub_rows, n_col, sub_cols, chans).transpose(
        1, 3, 0, 2, 4, 5
    )
    outgoing = outgoing.reshape(n_row * n_col, per_tile, sub_rows, sub_cols, chans)
    arrived = lax.all_to_all(outgoing, ("row", "col"), split_axis=0, concat_axis=0, tiled=True)
    arrived = arrived.reshape(n_row, 8, col_tiles, per_tile, sub_rows, sub_cols, chans)
    grouped = arrived.transpose(2, 4, 5, 0, 3, 1, 6).reshape(n_groups, 64, chans)
    attended = attend(grouped, qkv_grid, out_grid)
    attended = attended.reshape(col_tiles, sub_rows, sub_cols, n_row, per_tile, 8, chans)
    returning = attended.transpose(3, 5, 0, 4, 1, 2, 6).reshape(
        n_row * n_col, per_tile, sub_rows, sub_cols, chans
    )
    home = lax.all_to_all(returning, ("row", "col"), split_axis=0, concat_axis=0, tiled=True)
    home = home.reshape(n_row, n_col, per_tile, sub_rows, sub_cols, chans).transpose(
        2, 0, 3, 1, 4, 5
    )
    result = home.reshape(tile_h, tile_w, chans)
    return result


def solution(mesh):
    placed = (P("row", "col", None), P(), P(), P(), P(), P(), P(), P())
    return jax.shard_map(
        on_device, mesh=mesh, in_specs=placed, out_specs=P("row", "col", None), check_vma=False
    )
```

profile of v0, /device:TPU:0, one launch (start us, length us, event | category | flops | bytes accessed | tf_op | source)
XLA Modules:
  0.0 363.1 jit_solution(10244235552004134760)
XLA Ops:
  0.0 2.1 convert_reduce_fusion
  2.1 2.5 fusion.36
  4.7 40.8 %fusion.4 = bf16[32,64,2048]{2,1,0:T(8,128)(2,1)S(1)} fusion(bf16[32,64,512]{2,1,0:T(8,128)(2,1)} %param.8, bf16[512,2048]{1,0:T(8,128)(2,1)S(1)} %copy-done, f32[32,64]{1,0:T(8,128)S(1)} %add_rsqrt_fusion.2, f32[32,64]{1,0:T(8,128)S(1)} %broadcast_multiply_fusion.2), kind=kOutput, calls=%fused_computation.6 | convolution fusion | flops 4571791360 | bytes 12599296 | tf_op jit(solution)/shard_map/rwc,cd->rwd/dot_general | solution.py:35
  45.5 1.3 collective-permute-start
  46.8 1.3 collective-permute-start.1
  48.1 6.3 %collective-permute-done.1 = bf16[1,64,2048]{2,1,0:T(8,128)(2,1)S(1)} collective-permute-done((bf16[1,64,2048]{2,1,0:T(8,128)(2,1)S(1)}, bf16[1,64,2048]{2,1,0:T(8,128)(2,1)S(1)}, u32[]{:S(2)}, u32[]{:S(2)}) %collective-permute-start.1) | collective-permute-done | bytes 262176 | tf_op jit(solution)/shard_map/ppermute | solution.py:19
  54.4 0.5 pad_maximum_fusion.5
  54.9 3.2 collective-permute-start.2
  58.1 1.5 collective-permute-start.3
  59.7 2.4 collective-permute-done.2
  62.2 4.4 %collective-permute-done.3 = bf16[34,1,2048]{2,1,0:T(2,128)(2,1)S(1)} collective-permute-done((bf16[34,1,2048]{2,1,0:T(2,128)(2,1)S(1)}, bf16[34,1,2048]{2,1,0:T(2,128)(2,1)S(1)}, u32[]{:S(2)}, u32[]{:S(2)}) %collective-permute-start.3) | collective-permute-done | bytes 139296 | tf_op jit(solution)/shard_map/ppermute | solution.py:19
  66.6 9.1 %maximum_maximum_fusion = (bf16[34,65,2048]{2,1,0:T(8,128)(2,1)S(1)}, bf16[34,65,2048]{2,1,0:T(8,128)(2,1)}) fusion(bf16[1,64,2048]{2,1,0:T(8,128)(2,1)S(1)} %collective-permute-done.1, bf16[32,64,2048]{2,1,0:T(8,128)(2,1)S(1)} %fusion.4, bf16[1,64,2048]{2,1,0:T(8,128)(2,1)S(1)} %collective-permute-done, bf16[34,1,2048]{2,1,0:T(2,128)(2,1)S(1)} %collective-permute-done.2, ...), kind=kLoop, calls=%fused_computation.49 | loop fusion | flops 72417280 | bytes 27295744 | tf_op jit(solution)/shard_map/concatenate | solution.py:15
  75.7 61.6 %fusion.38 = bf16[32,64,512]{2,1,0:T(8,128)(2,1)S(1)} fusion(bf16[32,64,512]{2,1,0:T(8,128)(2,1)S(1)} %copy-done.3, bf16[2048,512]{1,0:T(8,128)(2,1)S(1)} %copy-done.7, bf16[32,64,2048]{2,1,0:T(8,128)(2,1)S(1)} %fusion.4, bf16[34,65,2048]{2,1,0:T(8,128)(2,1)} %get-tuple-element.6, bf16[1,64,2048]{2,1,0:T(8,128)(2,1)S(1)} %collective-permute-done.1, ...), kind=kOutput, calls=%fused_computation.67 | convolution fusion | flops 4688183296 | bytes 65609728 | tf_op jit(solution)/shard_map/rwd,dc->rwc/dot_general | solution.py:75
  137.7 2.5 convert_bitcast_fusion.1
  140.2 0.9 multiply_reduce_fusion.3
  141.3 4.8 %copy.131 = f32[4,8,8,8,512]{4,3,2,1,0:T(8,128)} copy(f32[4,8,8,8,512]{4,3,1,2,0:T(8,128)} %convert_bitcast_fusion.1) | data formatting | bytes 8388608 | tf_op jit(solution)/shard_map/convert_element_type | solution.py:60
  146.2 5.7 %convolution_convert_fusion.1 = bf16[32,64,1536]{2,1,0:T(8,128)(2,1)S(1)} fusion(f32[32,64,512]{2,1,0:T(8,128)} %bitcast.97, f32[32,64]{1,0:T(8,128)S(1)} %rsqrt.32, f32[32,64]{1,0:T(8,128)S(1)} %div.41, bf16[512,1536]{1,0:T(8,128)(2,1)S(1)} %copy-done.8), kind=kOutput, calls=%fused_computation.62 | convolution fusion | flops 3227516928 | bytes 12075008 | tf_op jit(solution)/shard_map/gtc,cd->gtd/dot_general | solution.py:43
  151.9 2.8 fusion.102
  154.8 4.8 %copy.135 = bf16[32,64,512]{1,2,0:T(8,128)(2,1)} copy(bf16[32,64,512]{2,1,0:T(8,128)(2,1)} %get-tuple-element.15) | data formatting | bytes 4194304 | tf_op jit(solution)/shard_map/slice | solution.py:46
  159.6 4.9 %copy.136 = bf16[32,64,512]{1,2,0:T(8,128)(2,1)} copy(bf16[32,64,512]{2,1,0:T(8,128)(2,1)} %get-tuple-element.14) | data formatting | bytes 4194304 | tf_op jit(solution)/shard_map/slice | solution.py:47
  164.5 3.2 copy.134
  167.6 12.3 %fusion.104 = (f32[32,16,64]{2,1,0:T(8,128)S(1)}, f32[32,16,64,64]{2,3,1,0:T(8,128)}) fusion(bf16[32,64,16,32]{1,3,2,0:T(8,128)(2,1)} %bitcast.108, bf16[32,64,16,32]{1,3,2,0:T(8,128)(2,1)} %bitcast.110), kind=kOutput, calls=%fused_computation.142 | convolution fusion | flops 140509248 | bytes 12713984 | tf_op jit(solution)/shard_map/sub | solution.py:52
  180.0 11.5 %fusion.40 = bf16[32,16,32,64]{3,2,1,0:T(8,128)(2,1)} fusion(bf16[32,64,16,32]{1,3,2,0:T(8,128)(2,1)} %bitcast.111, f32[32,16,64,64]{2,3,1,0:T(8,128)} %get-tuple-element.27, f32[32,16,64]{2,1,0:T(8,128)S(1)} %get-tuple-element.26), kind=kOutput, calls=%fused_computation.77 | convolution fusion | flops 139460608 | bytes 12713984 | tf_op jit(solution)/shard_map/ghqk,gkhd->gqhd/dot_general | solution.py:55
  191.5 3.5 add_convert_fusion.1
  195.3 2.2 reshape_reshape.3
  197.5 2.1 copy.140
  199.6 2.2 copy.141
  201.8 48.9 %all_to_all.10 = bf16[128,2,4,2,512]{4,3,2,1,0:T(2,128)(2,1)S(1)} all-to-all(bf16[128,2,4,2,512]{4,3,2,1,0:T(2,128)(2,1)S(1)} %copy.141), channel_id=1, replica_groups=mesh['row'=4,'col'=32] {'row','col'}, dimensions={0} | all-to-all | bytes 4194304 | tf_op jit(solution)/shard_map/all_to_all | solution.py:95
  250.7 2.1 fusion.42
  252.8 0.9 copy.143
  253.7 0.9 copy.145
  254.7 4.2 %multiply_reduce_fusion.2 = f32[4,4,2,4,2,8]{2,1,4,0,5,3:T(4,128)S(1)} fusion(bf16[4,8,4,2,4,2,512]{6,5,4,3,2,1,0:T(2,128)(2,1)S(1)} %bitcast.93, f32[4,4,2,4,2,8]{2,1,4,0,5,3:T(4,128)S(1)} %copy.145), kind=kLoop, calls=%fused_computation.72 | loop fusion | flops 4192256 | bytes 2113536 | tf_op jit(solution)/shard_map/reduce_sum | solution.py:29
  258.9 0.9 copy.146
  260.1 2.1 convert_bitcast_fusion
  262.2 4.4 %copy.142 = f32[4,4,2,4,2,8,512]{6,5,4,3,2,1,0:T(8,128)} copy(f32[4,4,2,4,2,8,512]{6,2,1,4,0,5,3:T(2,128)S(1)} %convert_bitcast_fusion) | data formatting | bytes 8388608 | tf_op jit(solution)/shard_map/convert_element_type | solution.py:60
  266.7 6.2 %convolution_convert_fusion = bf16[32,64,1536]{2,1,0:T(8,128)(2,1)S(1)} fusion(f32[32,64,512]{2,1,0:T(8,128)} %bitcast.99, f32[32,64]{1,0:T(8,128)S(1)} %rsqrt.34, f32[32,64]{1,0:T(8,128)S(1)} %div.46, bf16[512,1536]{1,0:T(8,128)(2,1)} %param.14), kind=kOutput, calls=%fused_computation.61 | convolution fusion | flops 3227516928 | bytes 12075008 | tf_op jit(solution)/shard_map/gtc,cd->gtd/dot_general | solution.py:43
  272.9 2.8 fusion.101
  275.8 4.8 %copy.149 = bf16[32,64,512]{1,2,0:T(8,128)(2,1)} copy(bf16[32,64,512]{2,1,0:T(8,128)(2,1)} %get-tuple-element.12) | data formatting | bytes 4194304 | tf_op jit(solution)/shard_map/slice | solution.py:46
  280.6 4.9 %copy.150 = bf16[32,64,512]{1,2,0:T(8,128)(2,1)} copy(bf16[32,64,512]{2,1,0:T(8,128)(2,1)} %get-tuple-element.11) | data formatting | bytes 4194304 | tf_op jit(solution)/shard_map/slice | solution.py:47
  285.5 3.2 copy.148
  288.6 12.4 %fusion.105 = (f32[32,16,64]{2,1,0:T(8,128)S(1)}, f32[32,16,64,64]{2,3,1,0:T(8,128)}) fusion(bf16[32,64,16,32]{1,3,2,0:T(8,128)(2,1)} %bitcast.109, bf16[32,64,16,32]{1,3,2,0:T(8,128)(2,1)} %bitcast.112), kind=kOutput, calls=%fused_computation.143 | convolution fusion | flops 140509248 | bytes 12713984 | tf_op jit(solution)/shard_map/sub | solution.py:52
  301.1 11.5 %fusion.39 = bf16[32,16,32,64]{3,2,1,0:T(8,128)(2,1)} fusion(bf16[32,64,16,32]{1,3,2,0:T(8,128)(2,1)} %bitcast.113, f32[32,16,64,64]{2,3,1,0:T(8,128)} %get-tuple-element.29, f32[32,16,64]{2,1,0:T(8,128)S(1)} %get-tuple-element.28), kind=kOutput, calls=%fused_computation.76 | convolution fusion | flops 139460608 | bytes 12713984 | tf_op jit(solution)/shard_map/ghqk,gkhd->gqhd/dot_general | solution.py:55
  312.5 4.8 %add_convert_fusion = bf16[32,64,512]{2,1,0:T(8,128)(2,1)S(1)} fusion(f32[32,64,512]{2,1,0:T(8,128)} %bitcast.100, bf16[32,64,512]{1,2,0:T(8,128)(2,1)} %bitcast.115, bf16[512,512]{1,0:T(8,128)(2,1)S(1)} %copy-done.5), kind=kOutput, calls=%fused_computation.70 | convolution fusion | flops 1075838976 | bytes 8912896 | tf_op jit(solution)/shard_map/gtc,cd->gtd/dot_general | solution.py:59
  317.3 2.2 copy.153
  319.5 34.4 %all_to_all.11 = bf16[128,2,4,2,512]{4,3,2,1,0:T(2,128)(2,1)S(1)} all-to-all(bf16[128,2,4,2,512]{4,3,2,1,0:T(2,128)(2,1)S(1)} %bitcast.104), channel_id=1, replica_groups=mesh['row'=4,'col'=32] {'row','col'}, dimensions={0} | all-to-all | bytes 4194304 | tf_op jit(solution)/shard_map/all_to_all | solution.py:103
  353.8 1.2 copy.154
  355.0 3.5 copy.155
  358.5 4.1 %reshape.145 = bf16[32,64,512]{2,1,0:T(8,128)(2,1)} reshape(bf16[2,4,4,32,2,512]{5,4,3,2,1,0:T(2,128)(2,1)} %copy.155) | data formatting | bytes 4194304 | tf_op jit(solution)/shard_map/reshape | solution.py:107
  (37 shorter events, 1.7 us)
Async XLA Ops:
  0.0 4.6 %copy-start = (bf16[512,2048]{1,0:T(8,128)(2,1)S(1)}, bf16[512,2048]{1,0:T(8,128)(2,1)}, u32[]{:S(2)}) copy-start(bf16[512,2048]{1,0:T(8,128)(2,1)} %param.9) | copy-start | bytes 6291460
  4.6 55.0 %copy-start.6 = (f32[3,3,2048]{2,1,0:T(4,128)S(1)}, f32[3,3,2048]{2,1,0:T(4,128)}, u32[]{:S(2)}) copy-start(f32[3,3,2048]{2,1,0:T(4,128)} %param.10) | copy-start | bytes 221188
  45.5 2.6 collective-permute-start
  46.8 7.6 %collective-permute-start.1 = (bf16[1,64,2048]{2,1,0:T(8,128)(2,1)S(1)}, bf16[1,64,2048]{2,1,0:T(8,128)(2,1)S(1)}, u32[]{:S(2)}, u32[]{:S(2)}) collective-permute-start(bf16[1,64,2048]{2,1,0:T(8,128)(2,1)S(1)} %get-tuple-element.10), channel_id=1, source_target_pairs={{32,0},{64,32},{96,64},{33,1},{65,33},{97,65},{34,2},{66,34},{98,6... | collective-permute-start | bytes 786440 | tf_op jit(solution)/shard_map/ppermute | solution.py:19
  54.9 20.8 %copy-start.3 = (bf16[32,64,512]{2,1,0:T(8,128)(2,1)S(1)}, bf16[32,64,512]{2,1,0:T(8,128)(2,1)}, u32[]{:S(2)}) copy-start(bf16[32,64,512]{2,1,0:T(8,128)(2,1)} %param.8) | copy-start | bytes 6291460
  54.9 20.8 %copy-start.7 = (bf16[2048,512]{1,0:T(8,128)(2,1)S(1)}, bf16[2048,512]{1,0:T(8,128)(2,1)}, u32[]{:S(2)}) copy-start(bf16[2048,512]{1,0:T(8,128)(2,1)} %param.11) | copy-start | bytes 6291460
  54.9 7.2 %collective-permute-start.2 = (bf16[34,1,2048]{2,1,0:T(2,128)(2,1)S(1)}, bf16[34,1,2048]{2,1,0:T(2,128)(2,1)S(1)}, u32[]{:S(2)}, u32[]{:S(2)}) collective-permute-start(bf16[34,1,2048]{2,1,0:T(2,128)(2,1)S(1)} %get-tuple-element.7), channel_id=1, source_target_pairs={{0,1},{1,2},{2,3},{3,4},{4,5},{5,6},{6,7},{7,8},{8,9},{9,10},{10,1... | collective-permute-start | bytes 417800 | tf_op jit(solution)/shard_map/ppermute | solution.py:17
  58.1 8.4 %collective-permute-start.3 = (bf16[34,1,2048]{2,1,0:T(2,128)(2,1)S(1)}, bf16[34,1,2048]{2,1,0:T(2,128)(2,1)S(1)}, u32[]{:S(2)}, u32[]{:S(2)}) collective-permute-start(bf16[34,1,2048]{2,1,0:T(2,128)(2,1)S(1)} %get-tuple-element.8), channel_id=1, source_target_pairs={{1,0},{2,1},{3,2},{4,3},{5,4},{6,5},{7,6},{8,7},{9,8},{10,9},{11,1... | collective-permute-start | bytes 417800 | tf_op jit(solution)/shard_map/ppermute | solution.py:19
  137.3 8.9 %copy-start.8 = (bf16[512,1536]{1,0:T(8,128)(2,1)S(1)}, bf16[512,1536]{1,0:T(8,128)(2,1)}, u32[]{:S(2)}) copy-start(bf16[512,1536]{1,0:T(8,128)(2,1)} %param.12) | copy-start | bytes 4718596
  180.0 11.5 %copy-start.2 = (f32[4,8,8,8,512]{4,3,2,1,0:T(8,128)S(1)}, f32[4,8,8,8,512]{4,3,2,1,0:T(8,128)}, u32[]{:S(2)}) copy-start(f32[4,8,8,8,512]{4,3,2,1,0:T(8,128)} %copy.131) | copy-start | bytes 12582916
  180.0 11.5 %copy-start.4 = (bf16[512,512]{1,0:T(8,128)(2,1)S(1)}, bf16[512,512]{1,0:T(8,128)(2,1)}, u32[]{:S(2)}) copy-start(bf16[512,512]{1,0:T(8,128)(2,1)} %param.13) | copy-start | bytes 1572868
  301.0 11.5 %copy-start.5 = (bf16[512,512]{1,0:T(8,128)(2,1)S(1)}, bf16[512,512]{1,0:T(8,128)(2,1)}, u32[]{:S(2)}) copy-start(bf16[512,512]{1,0:T(8,128)(2,1)} %param.15) | copy-start | bytes 1572868
  301.0 61.6 %copy-start.1 = (bf16[512,2048]{1,0:T(8,128)(2,1)S(1)}, bf16[512,2048]{1,0:T(8,128)(2,1)}, u32[]{:S(2)}) copy-start(bf16[512,2048]{1,0:T(8,128)(2,1)} %param.9) | copy-start | bytes 6291460
where the time goes:
time: 370 us; the launch traced here: 363 us
  matrix products  170 us (46%)
  blocking collectives  83.3 us (23%)
  local copies, waits for them, and re-layouts  61.7 us (17%)
  other arithmetic  26.6 us (7%)
  waiting for transfers between devices  13.2 us (4%)
  starting transfers between devices  7.31 us (2%)
    dot_general x1, matrix products, on_device(): jnp.einsum('rwd,dc->rwc', spatial, w_project, preferred_element_type=jnp....  61.6 us
    all_to_all x1, blocking collectives, on_device(): lax.all_to_all(outgoing, ('row', 'col'), split_axis=0, concat_axis=0, til...  48.9 us
    dot_general x1, matrix products, expand(): jnp.einsum('rwc,cd->rwd', normed, w_expand, preferred_element_type=jnp.fl...  40.8 us
    all_to_all x1, blocking collectives, on_device(): lax.all_to_all(returning, ('row', 'col'), split_axis=0, concat_axis=0, ti...  34.4 us
    sub x2, matrix products, attend(): scores = scores - jnp.max(scores, axis=-1, keepdims=True)  24.8 us
    dot_general x2, matrix products, attend(): jnp.einsum('ghqk,gkhd->gqhd', weights, values, preferred_element_type=jnp...  23 us
    slice x4, local copies, waits for them, and re-layouts, attend(): keys = proj[:, :, width:2 * width].reshape(groups, count, HEADS, head_dim)  15.4 us
    dot_general x2, matrix products, attend(): jnp.einsum('gtc,cd->gtd', normed, qkv, preferred_element_type=jnp.float32)  11.8 us
  transfers between devices with their start and end apart: 4, of which 3 were waited for; matrix products, arithmetic and copies ran while one was open for 0% of the time, Pallas kernels for 0%

commit v1 on v0

v1 whole, which is shorter than its diff:
```python
import functools

import jax
import jax.numpy as jnp
import numpy as np
from jax import lax
from jax.experimental import pallas as pl
from jax.experimental.pallas import tpu as pltpu
from jax.sharding import PartitionSpec as P

BF16 = jnp.bfloat16
F32 = jnp.float32
HEAD = 32
CHANS = 512
WIDE = 2048
CB = 512
VMEM_LIMIT = 56 * 2**20
SCALE_LOG2 = float(HEAD**-0.5 * np.log2(np.e))


def layer_norm(v):
    mean = jnp.mean(v, axis=-1, keepdims=True)
    cent = v - mean
    var = jnp.mean(cent * cent, axis=-1, keepdims=True)
    return (cent * lax.rsqrt(var + 1e-05)).astype(BF16)


def gelu(v):
    half = 0.5 * v
    return half + half * lax.erf(v * 0.7071067811865476)


def mm(a, b):
    return lax.dot_general(a, b, (((1,), (0,)), ((), ())), preferred_element_type=F32)


def mm_nt(a, b):
    return lax.dot_general(a, b, (((1,), (1,)), ((), ())), preferred_element_type=F32)


def permutation(dims, order):
    count = int(np.prod(dims))
    source = np.arange(count).reshape(dims).transpose(order).reshape(-1)
    matrix = np.zeros((count, count), np.float32)
    matrix[np.arange(count), source] = 1.0
    return jnp.asarray(matrix, BF16)


def whole(shape):
    zeros = (0,) * len(shape)
    return pl.BlockSpec(shape, lambda *_: zeros)


def params():
    return pltpu.CompilerParams(vmem_limit_bytes=VMEM_LIMIT)


def expand_kernel(x_ref, w_ref, perm_ref, xp_ref, hid_ref, normed):
    for pair in range(2):
        rows = x_ref[:, 2 * pair : 2 * pair + 2].reshape(256, CHANS)
        moved = mm(perm_ref[...], rows)
        xp_ref[2 * pair : 2 * pair + 2] = moved.astype(BF16).reshape(2, 8, 16, CHANS)
        normed[256 * pair : 256 * pair + 256] = layer_norm(moved)
    for at in range(0, WIDE, 256):
        pre = mm(normed[...], w_ref[:, at : at + 256])
        hid_ref[:, :, :, at : at + 256] = gelu(pre).astype(BF16).reshape(4, 8, 16, 256)


def expand(field, w_expand, part):
    return pl.pallas_call(
        expand_kernel,
        grid=(2,),
        in_specs=[
            pl.BlockSpec((2, 4, 64, CHANS), lambda s: (0, 2 * part + s, 0, 0)),
            whole((CHANS, WIDE)),
            whole((256, 256)),
        ],
        out_specs=[
            pl.BlockSpec((4, 8, 16, CHANS), lambda s: (s, 0, 0, 0)),
            pl.BlockSpec((4, 8, 16, WIDE), lambda s: (s, 0, 0, 0)),
        ],
        out_shape=[
            jax.ShapeDtypeStruct((8, 8, 16, CHANS), BF16),
            jax.ShapeDtypeStruct((8, 8, 16, WIDE), BF16),
        ],
        scratch_shapes=[pltpu.VMEM((512, CHANS), BF16)],
        compiler_params=params(),
        cost_estimate=pl.CostEstimate(
            flops=2 * 1024 * CHANS * WIDE, bytes_accessed=8 * 2**20, transcendentals=1024 * WIDE
        ),
        name="expand",
    )(field.reshape(2, 16, 64, CHANS), w_expand, permutation((2, 2, 8, 8), (1, 3, 0, 2)))


def mix_kernel(
    part, hid_ref, prev_ref, next_ref, xp_ref, top_ref, bot_ref, left_ref, right_ref, we_ref, dw_ref, wp_ref, perm_ref,
    out_ref, pad, normed, rim, spatial, acc,
):
    step = pl.program_id(0)

    @pl.when(step == 0)
    def _():
        both = jnp.concatenate([layer_norm(top_ref[...].astype(F32)), layer_norm(bot_ref[...].astype(F32))], axis=0)
        normed[0:128] = mm(perm_ref[...], both).astype(BF16)
        normed[128:176] = layer_norm(left_ref[...].astype(F32))
        normed[176:224] = layer_norm(right_ref[...].astype(F32))
        acc[...] = jnp.zeros_like(acc)

    for at in range(0, CB, 256):
        rim[:, at : at + 256] = gelu(mm(normed[...], we_ref[:, at : at + 256])).astype(BF16).astype(F32)
    pad[1:9, 1:9] = hid_ref[...]
    for j in range(8):
        before = prev_ref[0, j]
        after = next_ref[0, j]
        if part == 0:
            before = jnp.concatenate([rim[16 * j : 16 * j + 8], before.astype(F32)[0:8]], axis=0).astype(BF16)
        else:
            after = jnp.concatenate([after.astype(F32)[8:16], rim[16 * j + 8 : 16 * j + 16]], axis=0).astype(BF16)
        pad[0, 1 + j] = before
        pad[9, 1 + j] = after
    sub = lax.broadcasted_iota(jnp.int32, (8, CB), 0)
    for row in range(10):
        at = 128 + 8 * part + row
        last = pad[row, 8].astype(F32)
        first = pad[row, 1].astype(F32)
        west, east = [], []
        for b in range(2):
            turned = pltpu.roll(last[8 * b : 8 * b + 8], 1, 0)
            west.append(jnp.where(sub == 0, rim[at + 16 * b : at + 16 * b + 1], turned))
            turned = pltpu.roll(first[8 * b : 8 * b + 8], 7, 0)
            east.append(jnp.where(sub == 7, rim[at + 48 + 16 * b : at + 48 + 16 * b + 1], turned))
        pad[row, 0] = jnp.concatenate(west, axis=0).astype(BF16)
        pad[row, 9] = jnp.concatenate(east, axis=0).astype(BF16)

    for pair in range(4):
        for lane in range(0, CB, 128):
            taps = [dw_ref[t : t + 1, lane : lane + 128].astype(BF16) for t in range(9)]
            for i in (2 * pair, 2 * pair + 1):
                for j in range(8):
                    total = None
                    for t in range(9):
                        term = pad[i + t // 3, j + t % 3, :, lane : lane + 128] * taps[t]
                        total = term if total is None else total + term
                    spatial[i, j, :, lane : lane + 128] = gelu(total.astype(F32)).astype(BF16)
        rows = slice(256 * pair, 256 * pair + 256)
        acc[rows] += mm(spatial[2 * pair : 2 * pair + 2].reshape(256, CB), wp_ref[...])

    @pl.when(step == WIDE // CB - 1)
    def _():
        x = xp_ref[...].reshape(1024, CHANS).astype(F32)
        out_ref[...] = (x + acc[...]).astype(BF16).reshape(64, 16, CHANS)


def mix(part, hid, hid_other, xp, rims, w_expand, dw, w_project):
    edges = (7, 0)
    hid_spec = pl.BlockSpec((8, 8, 16, CB), lambda s: (0, 0, 0, s))
    edge_spec = [pl.BlockSpec((1, 8, 16, CB), lambda s, e=e: (e, 0, 0, s)) for e in edges]
    return pl.pallas_call(
        functools.partial(mix_kernel, part),
        grid=(WIDE // CB,),
        in_specs=[
            hid_spec,
            edge_spec[0],
            edge_spec[1],
            whole((8, 8, 16, CHANS)),
            whole((64, CHANS)),
            whole((64, CHANS)),
            whole((48, CHANS)),
            whole((48, CHANS)),
            pl.BlockSpec((CHANS, CB), lambda s: (0, s)),
            pl.BlockSpec((9, CB), lambda s: (0, s)),
            pl.BlockSpec((CB, CHANS), lambda s: (s, 0)),
            whole((128, 128)),
        ],
        out_specs=whole((64, 16, CHANS)),
        out_shape=jax.ShapeDtypeStruct((64, 16, CHANS), BF16),
        scratch_shapes=[
            pltpu.VMEM((10, 10, 16, CB), BF16),
            pltpu.VMEM((224, CHANS), BF16),
            pltpu.VMEM((224, CB), F32),
            pltpu.VMEM((8, 8, 16, CB), BF16),
            pltpu.VMEM((1024, CHANS), F32),
        ],
        compiler_params=params(),
        cost_estimate=pl.CostEstimate(
            flops=2 * 1024 * CHANS * WIDE, bytes_accessed=8 * 2**20, transcendentals=1024 * WIDE
        ),
        name="mix",
    )(hid, hid_other, hid_other, xp, *rims, w_expand, dw, w_project, permutation((2, 8, 8), (2, 0, 1)))


def segment_max(scores):
    low = lax.broadcasted_iota(jnp.int32, (1, 128), 1) < 64
    found = []
    for at in range(0, scores.shape[1], 128):
        v = scores[:, at : at + 128]
        first = jnp.max(jnp.where(low, v, -jnp.inf), axis=-1, keepdims=True)
        second = jnp.max(jnp.where(low, -jnp.inf, v), axis=-1, keepdims=True)
        found.append(jnp.where(low, first, second))
    return jnp.concatenate(found, axis=1)


def attend_kernel(home, x_ref, wqkv_ref, wo_ref, turn_ref, mask_ref, out_ref, grouped, proj, context):
    for t in range(4):
        moved = mm(turn_ref[...], x_ref[16 * t : 16 * t + 16].reshape(256, CHANS))
        grouped[:, 16 * t : 16 * t + 16] = moved.astype(BF16).reshape(16, 16, CHANS)
    mask = mask_ref[...]
    for b in range(2):
        x = grouped[8 * b : 8 * b + 8].reshape(512, CHANS).astype(F32)
        proj[...] = mm(layer_norm(x), wqkv_ref[...]).astype(BF16)
        for g in range(8):
            rows = slice(64 * g, 64 * g + 64)
            for at in range(0, CHANS, 128):
                query = proj[rows, at : at + 128]
                keys = jnp.concatenate([proj[rows, CHANS + at : CHANS + at + 128]] * 4, axis=0) * mask
                values = jnp.concatenate([proj[rows, 2 * CHANS + at : 2 * CHANS + at + 128]] * 4, axis=0) * mask
                scores = mm_nt(query, keys)
                weights = jnp.exp2((scores - segment_max(scores)) * SCALE_LOG2).astype(BF16)
                both = mm(weights, jnp.concatenate([values, mask], axis=1))
                context[rows, at : at + 128] = (both[:, :128] / both[:, 128:]).astype(BF16)
        done = x + mm(context[...], wo_ref[...])
        if home:
            grouped[8 * b : 8 * b + 8] = done.astype(BF16).reshape(8, 64, CHANS)
        else:
            done = done.reshape(4, 2, 8, 8, CHANS)
            for i in range(8):
                out_ref[i, :, b] = done[:, :, i].reshape(4, 16, CHANS).astype(BF16)
    if home:
        for t in range(4):
            moved = mm(turn_ref[...], grouped[:, 16 * t : 16 * t + 16].reshape(256, CHANS))
            out_ref[16 * t : 16 * t + 16] = moved.astype(BF16).reshape(16, 16, CHANS)


def attend(home, x, qkv, out_proj):
    heads = jnp.asarray(np.arange(256)[:, None] // 64 == np.arange(128)[None] // 32, BF16)
    shape = (64, 16, CHANS) if home else (8, 4, 2, 16, CHANS)
    return pl.pallas_call(
        functools.partial(attend_kernel, home),
        grid=(1,),
        in_specs=[
            whole((64, 16, CHANS)),
            whole((CHANS, 3 * CHANS)),
            whole((CHANS, CHANS)),
            whole((256, 256)),
            whole((256, 128)),
        ],
        out_specs=whole(shape),
        out_shape=jax.ShapeDtypeStruct(shape, BF16),
        scratch_shapes=[
            pltpu.VMEM((16, 64, CHANS), BF16),
            pltpu.VMEM((512, 3 * CHANS), BF16),
            pltpu.VMEM((512, CHANS), BF16),
        ],
        compiler_params=params(),
        cost_estimate=pl.CostEstimate(
            flops=8 * 1024 * CHANS * CHANS, bytes_accessed=4 * 2**20, transcendentals=2**20
        ),
        name="attend",
    )(x, qkv, out_proj, permutation((16, 16), (1, 0)), heads)


def exchange(blocks, groups):
    return lax.all_to_all(blocks, ("row", "col"), 0, 0, axis_index_groups=groups, tiled=True)


def on_device(field, w_expand, dw_kernel, w_project, qkv_block, out_block, qkv_grid, out_grid):
    n_row, n_col = lax.axis_size("row"), lax.axis_size("col")
    down = [(i, i + 1) for i in range(n_row - 1)]
    up = [(i + 1, i) for i in range(n_row - 1)]
    top = lax.ppermute(field[31], "row", down)
    bottom = lax.ppermute(field[0], "row", up)
    fill = jnp.zeros((14, CHANS), BF16)

    def rim(column):
        return jnp.concatenate([top[column : column + 1], field[:, column], bottom[column : column + 1], fill], axis=0)

    left = lax.ppermute(rim(63), "col", [(i, i + 1) for i in range(n_col - 1)])
    right = lax.ppermute(rim(0), "col", [(i + 1, i) for i in range(n_col - 1)])
    rims = (top, bottom, left, right)
    parts = [expand(field, w_expand, part) for part in range(2)]
    dw = dw_kernel.reshape(9, WIDE)
    groups = [[32 * row + 4 * j + c for row in range(n_row) for j in range(8)] for c in range(4)]
    homes = []
    for part in range(2):
        xp, hid = parts[part]
        mixed = mix(part, hid, parts[1 - part][1], xp, rims, w_expand, dw, w_project)
        blocked = attend(False, mixed, qkv_block, out_block).reshape(32, 2, 16, CHANS)
        gathered = exchange(blocked, groups).reshape(64, 16, CHANS)
        attended = attend(True, gathered, qkv_grid, out_grid).reshape(32, 2, 16, CHANS)
        homes.append(exchange(attended, groups))
    home = jnp.stack(homes).reshape(2, 8, 4, 2, 16, CHANS)
    return home.transpose(3, 0, 1, 2, 4, 5).reshape(32, 64, CHANS)


def solution(mesh):
    placed = (P("row", "col", None), P(), P(), P(), P(), P(), P(), P())
    return jax.shard_map(
        on_device, mesh=mesh, in_specs=placed, out_specs=P("row", "col", None), check_vma=False
    )
```

time: 370 us -> 166 us (0.45); the launches traced: 363 us -> 164 us
  matrix products: 170 us -> 0 us
  Pallas kernels: 0 us -> 78.2 us
  blocking collectives: 83.3 us -> 23.9 us
  local copies, waits for them, and re-layouts: 61.7 us -> 5.02 us
  starting transfers between devices: 7.31 us -> 35.1 us
  other arithmetic: 26.6 us -> 0.28 us
  waiting for transfers between devices: 13.2 us -> 21.4 us
    dot_general x8 -> x0, matrix products: 145 us -> none  [the longest x1 61.6 us: on_device(): jnp.einsum('rwd,dc->rwc', spatial, w_project, preferred_element_type=jnp....]
    pallas_call x0 -> x8, Pallas kernels: none -> 78.2 us  [the longest x4 36 us: attend(): pl.pallas_call(functools.partial(attend_kernel, home), grid=(1,), in_spec...]
    all_to_all x2 -> x1, blocking collectives: 83.3 us -> 23.9 us  [exchange(): lax.all_to_all(blocks, ('row', 'col'), 0, 0, axis_index_groups=groups, ti...]
    slice x10 -> x3, local copies, waits for them, and re-layouts: 31.5 us -> 1.15 us  [the longest x1 1.14 us: rim(): field[:, column]]
    all_to_all x0 -> x3, starting transfers between devices: none -> 24.8 us  [exchange(): lax.all_to_all(blocks, ('row', 'col'), 0, 0, axis_index_groups=groups, ti...]
    sub x2 -> x0, matrix products: 24.8 us -> none  [attend(): scores = scores - jnp.max(scores, axis=-1, keepdims=True)]
    all_to_all x0 -> x3, waiting for transfers between devices: none -> 21.4 us  [exchange(): lax.all_to_all(blocks, ('row', 'col'), 0, 0, axis_index_groups=groups, ti...]
    ppermute x4, waiting for transfers between devices: 13.2 us -> 0.01 us  [the longest x1 0.01 us: on_device(): bottom = lax.ppermute(field[0], 'row', up)]
  transfers between devices with their start and end apart: 4 -> 7, of which waited for: 3 -> 2; matrix products, arithmetic and copies ran while one was open for 0% -> 1% of each run, Pallas kernels for 0% -> 34%
where the time goes in v1:
time: 166 us; the launch traced here: 164 us
  Pallas kernels  78.2 us (47%)
  starting transfers between devices  35.1 us (21%)
  blocking collectives  23.9 us (14%)
  waiting for transfers between devices  21.4 us (13%)
  local copies, waits for them, and re-layouts  5.02 us (3%)
    pallas_call x4, Pallas kernels, attend(): pl.pallas_call(functools.partial(attend_kernel, home), grid=(1,), in_spec...  36 us
    pallas_call x2, Pallas kernels, mix(): pl.pallas_call(functools.partial(mix_kernel, part), grid=(WIDE // CB,), i...  28.1 us
    all_to_all x3, starting transfers between devices, exchange(): lax.all_to_all(blocks, ('row', 'col'), 0, 0, axis_index_groups=groups, ti...  24.8 us
    all_to_all x1, blocking collectives, exchange(): lax.all_to_all(blocks, ('row', 'col'), 0, 0, axis_index_groups=groups, ti...  23.9 us
    all_to_all x3, waiting for transfers between devices, exchange(): lax.all_to_all(blocks, ('row', 'col'), 0, 0, axis_index_groups=groups, ti...  21.4 us
    pallas_call x2, Pallas kernels, expand(): pl.pallas_call(expand_kernel, grid=(2,), in_specs=[pl.BlockSpec((2, 4, 64...  14.1 us
    ppermute x1, starting transfers between devices, on_device(): left = lax.ppermute(rim(63), 'col', [(i, i + 1) for i in range(n_col - 1)])  4.68 us
  transfers between devices with their start and end apart: 7, of which 2 were waited for; matrix products, arithmetic and copies ran while one was open for 1% of the time, Pallas kernels for 34%

profile of v1, /device:TPU:0, one launch (start us, length us, event | category | flops | bytes accessed | tf_op | source)
XLA Modules:
  0.0 164.2 jit_solution(4576675904575968855)
XLA Ops:
  0.0 0.9 slice_bitcast_fusion
  0.9 1.3 collective-permute-start.1
  2.2 3.0 %collective-permute-start = (bf16[64,512]{1,0:T(8,128)(2,1)S(1)}, bf16[64,512]{1,0:T(8,128)(2,1)S(1)}, u32[]{:S(2)}, u32[]{:S(2)}) collective-permute-start(bf16[64,512]{1,0:T(8,128)(2,1)S(1)} %get-tuple-element.16), channel_id=1, source_target_pairs={{0,32},{32,64},{64,96},{1,33},{33,65},{65,97},{2,34},{34,66},{66,9... | collective-permute-start | bytes 196616 | tf_op jit(solution)/shard_map/ppermute | solution.py:270
  5.2 1.1 fusion
  6.4 7.0 %expand.3 = (bf16[8,8,16,512]{3,2,1,0:T(8,128)(2,1)}, bf16[8,8,16,2048]{3,2,1,0:T(8,128)(2,1)}) custom-call(bf16[2,16,64,512]{3,2,1,0:T(8,128)(2,1)} %bitcast.28, bf16[512,2048]{1,0:T(8,128)(2,1)} %we_ref.3, bf16[256,256]{1,0:T(8,128)(2,1)} %constant.10.clone.perm_ref), custom_call_target="tpu_custom_call" | custom-call | flops 2147483648 | bytes 8388608 | tf_op jit(solution)/shard_map/expand/pallas_call | solution.py:70
  13.4 0.1 pad.9.clone
  13.5 0.0 collective-permute-done.1.bot_ref
  13.5 0.0 copy-start.2
  13.5 0.0 collective-permute-done.top_ref
  13.5 0.0 copy-start.3
  13.5 0.1 maximum_maximum_fusion.1
  13.6 1.3 collective-permute-start.3
  14.9 0.0 copy-start.6
  14.9 4.7 %collective-permute-start.2 = (bf16[48,512]{1,0:T(8,128)(2,1)S(1)}, bf16[48,512]{1,0:T(8,128)(2,1)S(1)}, u32[]{:S(2)}, u32[]{:S(2)}) collective-permute-start(bf16[48,512]{1,0:T(8,128)(2,1)S(1)} %get-tuple-element.22), channel_id=1, source_target_pairs={{0,1},{1,2},{2,3},{3,4},{4,5},{5,6},{6,7},{7,8},{8,9},{9,10},{10,1... | collective-permute-start | bytes 147464 | tf_op jit(solution)/shard_map/ppermute | solution.py:277
  19.6 7.1 %expand.2 = (bf16[8,8,16,512]{3,2,1,0:T(8,128)(2,1)}, bf16[8,8,16,2048]{3,2,1,0:T(8,128)(2,1)}) custom-call(bf16[2,16,64,512]{3,2,1,0:T(8,128)(2,1)} %bitcast.29, bf16[512,2048]{1,0:T(8,128)(2,1)} %we_ref.3, bf16[256,256]{1,0:T(8,128)(2,1)} %constant.10.clone.perm_ref), custom_call_target="tpu_custom_call" | custom-call | flops 2147483648 | bytes 8388608 | tf_op jit(solution)/shard_map/expand/pallas_call | solution.py:70
  26.7 0.0 copy-done.2
  26.7 0.0 copy-done.3
  26.7 0.0 copy-done.6
  26.7 0.7 reshape.34.dw_ref
  27.4 0.0 collective-permute-done.3.right_ref
  27.4 0.0 copy-start.4
  27.4 0.0 collective-permute-done.2.left_ref
  27.4 0.0 copy-start.5
  27.4 0.6 copy-done.4
  28.0 0.0 copy-done.5
  28.1 14.0 %mix.2.x_ref = bf16[64,16,512]{2,1,0:T(8,128)(2,1)} custom-call(bf16[8,8,16,2048]{3,2,1,0:T(8,128)(2,1)} %get-tuple-element.9.hid_ref.prev_ref.next_ref, bf16[8,8,16,2048]{3,2,1,0:T(8,128)(2,1)} %get-tuple-element.10.prev_ref.next_ref.hid_ref, bf16[8,8,16,2048]{3,2,1,0:T(8,128)(2,1)} %get-tuple-element.10.prev_ref.next_ref.hid_ref, ...), custom_call_target="tpu_custom_call" | custom-call | flops 2147483648 | bytes 8388608 | tf_op jit(solution)/shard_map/mix/pallas_call | solution.py:158
  42.1 8.9 %attend.4 = bf16[8,4,2,16,512]{4,3,2,1,0:T(8,128)(2,1)} custom-call(bf16[64,16,512]{2,1,0:T(8,128)(2,1)} %mix.2.x_ref, bf16[512,1536]{1,0:T(8,128)(2,1)} %wqkv_ref.6, bf16[512,512]{1,0:T(8,128)(2,1)} %wo_ref.6, bf16[256,256]{1,0:T(8,128)(2,1)} %constant.13.clone.turn_ref, bf16[256,128]{1,0:T(8,128)(2,1)} %constant.12.clone.mask_ref), custom_call_target="tpu_custom_call" | custom-call | flops 2147483648 | bytes 4194304 | tf_op jit(solution)/shard_map/attend/pallas_call | solution.py:237
  51.0 10.9 %all-to-all-start = ((bf16[32,2,16,512]{3,2,1,0:T(8,128)(2,1)}), bf16[32,2,16,512]{3,2,1,0:T(8,128)(2,1)S(1)}, u32[]{:S(2)}, u32[]{:S(2)}) async-start(bf16[32,2,16,512]{3,2,1,0:T(8,128)(2,1)} %bitcast.23), calls=%async_computation | async-start | bytes 2097152 | tf_op jit(solution)/shard_map/all_to_all | solution.py:263
  61.9 14.1 %mix.3.x_ref = bf16[64,16,512]{2,1,0:T(8,128)(2,1)} custom-call(bf16[8,8,16,2048]{3,2,1,0:T(8,128)(2,1)} %get-tuple-element.10.prev_ref.next_ref.hid_ref, bf16[8,8,16,2048]{3,2,1,0:T(8,128)(2,1)} %get-tuple-element.9.hid_ref.prev_ref.next_ref, bf16[8,8,16,2048]{3,2,1,0:T(8,128)(2,1)} %get-tuple-element.9.hid_ref.prev_ref.next_ref, ...), custom_call_target="tpu_custom_call" | custom-call | flops 2147483648 | bytes 8388608 | tf_op jit(solution)/shard_map/mix/pallas_call | solution.py:158
  76.0 8.8 %attend.6 = bf16[8,4,2,16,512]{4,3,2,1,0:T(8,128)(2,1)} custom-call(bf16[64,16,512]{2,1,0:T(8,128)(2,1)} %mix.3.x_ref, bf16[512,1536]{1,0:T(8,128)(2,1)} %wqkv_ref.6, bf16[512,512]{1,0:T(8,128)(2,1)} %wo_ref.6, bf16[256,256]{1,0:T(8,128)(2,1)} %constant.13.clone.turn_ref, bf16[256,128]{1,0:T(8,128)(2,1)} %constant.12.clone.mask_ref), custom_call_target="tpu_custom_call" | custom-call | flops 2147483648 | bytes 4194304 | tf_op jit(solution)/shard_map/attend/pallas_call | solution.py:237
  84.7 0.0 all-to-all-done
  84.7 0.0 copy-start
  84.7 10.0 %all-to-all-start.2 = ((bf16[32,2,16,512]{3,2,1,0:T(8,128)(2,1)}), bf16[32,2,16,512]{3,2,1,0:T(8,128)(2,1)S(1)}, u32[]{:S(2)}, u32[]{:S(2)}) async-start(bf16[32,2,16,512]{3,2,1,0:T(8,128)(2,1)} %bitcast.26), calls=%async_computation.2 | async-start | bytes 2097152 | tf_op jit(solution)/shard_map/all_to_all | solution.py:263
  94.8 0.0 copy-done
  94.8 9.2 %attend.5 = bf16[64,16,512]{2,1,0:T(8,128)(2,1)} custom-call(bf16[64,16,512]{2,1,0:T(8,128)(2,1)} %bitcast.22, bf16[512,1536]{1,0:T(8,128)(2,1)} %wqkv_ref.7, bf16[512,512]{1,0:T(8,128)(2,1)} %wo_ref.7, bf16[256,256]{1,0:T(8,128)(2,1)} %constant.13.clone.turn_ref, bf16[256,128]{1,0:T(8,128)(2,1)} %constant.12.clone.mask_ref), custom_call_target="tpu_custom_call" | custom-call | flops 2147483648 | bytes 4194304 | tf_op jit(solution)/shard_map/attend/pallas_call | solution.py:237
  104.0 10.6 %all-to-all-done.2 = bf16[32,2,16,512]{3,2,1,0:T(8,128)(2,1)S(1)} async-done(((bf16[32,2,16,512]{3,2,1,0:T(8,128)(2,1)}), bf16[32,2,16,512]{3,2,1,0:T(8,128)(2,1)S(1)}, u32[]{:S(2)}, u32[]{:S(2)}) %all-to-all-start.2) | async-done | bytes 1048608 | tf_op jit(solution)/shard_map/all_to_all | solution.py:263
  114.6 0.0 copy-start.1
  114.6 3.9 %all-to-all-start.1 = ((bf16[32,2,16,512]{3,2,1,0:T(8,128)(2,1)}), bf16[32,2,16,512]{3,2,1,0:T(8,128)(2,1)S(1)}, u32[]{:S(2)}, u32[]{:S(2)}) async-start(bf16[32,2,16,512]{3,2,1,0:T(8,128)(2,1)} %bitcast.25), calls=%async_computation.1 | async-start | bytes 2097152 | tf_op jit(solution)/shard_map/all_to_all | solution.py:263
  118.5 0.0 copy-done.1
  118.5 9.2 %attend.7 = bf16[64,16,512]{2,1,0:T(8,128)(2,1)} custom-call(bf16[64,16,512]{2,1,0:T(8,128)(2,1)} %bitcast.24, bf16[512,1536]{1,0:T(8,128)(2,1)} %wqkv_ref.7, bf16[512,512]{1,0:T(8,128)(2,1)} %wo_ref.7, bf16[256,256]{1,0:T(8,128)(2,1)} %constant.13.clone.turn_ref, bf16[256,128]{1,0:T(8,128)(2,1)} %constant.12.clone.mask_ref), custom_call_target="tpu_custom_call" | custom-call | flops 2147483648 | bytes 4194304 | tf_op jit(solution)/shard_map/attend/pallas_call | solution.py:237
  127.7 10.8 %all-to-all-done.1 = bf16[32,2,16,512]{3,2,1,0:T(8,128)(2,1)S(1)} async-done(((bf16[32,2,16,512]{3,2,1,0:T(8,128)(2,1)}), bf16[32,2,16,512]{3,2,1,0:T(8,128)(2,1)S(1)}, u32[]{:S(2)}, u32[]{:S(2)}) %all-to-all-start.1) | async-done | bytes 1048608 | tf_op jit(solution)/shard_map/all_to_all | solution.py:263
  138.5 23.9 %all_to_all.20 = bf16[32,2,16,512]{3,2,1,0:T(8,128)(2,1)S(1)} all-to-all(bf16[32,2,16,512]{3,2,1,0:T(8,128)(2,1)} %bitcast.27), channel_id=1, replica_groups={{0,4,8,12,16,20,24,28,32,36,40,44,48,52,56,60,64,68,72,76,80,84,88,92,9..., dimensions={0} | all-to-all | bytes 2097152 | tf_op jit(solution)/shard_map/all_to_all | solution.py:263
  162.5 0.2 pad_maximum_fusion
  162.7 1.5 copy.25
  (4 shorter events, 0.0 us)
Async XLA Ops:
  0.9 12.6 %collective-permute-start.1 = (bf16[64,512]{1,0:T(8,128)(2,1)S(1)}, bf16[64,512]{1,0:T(8,128)(2,1)S(1)}, u32[]{:S(2)}, u32[]{:S(2)}) collective-permute-start(bf16[64,512]{1,0:T(8,128)(2,1)S(1)} %get-tuple-element.15), channel_id=1, source_target_pairs={{32,0},{64,32},{96,64},{33,1},{65,33},{97,65},{34,2},{66,34},{98,6... | collective-permute-start | bytes 196616 | tf_op jit(solution)/shard_map/ppermute | solution.py:271
  2.2 11.3 %collective-permute-start = (bf16[64,512]{1,0:T(8,128)(2,1)S(1)}, bf16[64,512]{1,0:T(8,128)(2,1)S(1)}, u32[]{:S(2)}, u32[]{:S(2)}) collective-permute-start(bf16[64,512]{1,0:T(8,128)(2,1)S(1)} %get-tuple-element.16), channel_id=1, source_target_pairs={{0,32},{32,64},{64,96},{1,33},{33,65},{65,97},{2,34},{34,66},{66,9... | collective-permute-start | bytes 196616 | tf_op jit(solution)/shard_map/ppermute | solution.py:270
  13.5 13.2 %copy-start.2 = (bf16[64,512]{1,0:T(8,128)(2,1)}, bf16[64,512]{1,0:T(8,128)(2,1)S(1)}, u32[]{:S(2)}) copy-start(bf16[64,512]{1,0:T(8,128)(2,1)S(1)} %collective-permute-done.1.bot_ref) | copy-start | bytes 196612
  13.5 13.2 %copy-start.3 = (bf16[64,512]{1,0:T(8,128)(2,1)}, bf16[64,512]{1,0:T(8,128)(2,1)S(1)}, u32[]{:S(2)}) copy-start(bf16[64,512]{1,0:T(8,128)(2,1)S(1)} %collective-permute-done.top_ref) | copy-start | bytes 196612
  13.6 13.8 %collective-permute-start.3 = (bf16[48,512]{1,0:T(8,128)(2,1)S(1)}, bf16[48,512]{1,0:T(8,128)(2,1)S(1)}, u32[]{:S(2)}, u32[]{:S(2)}) collective-permute-start(bf16[48,512]{1,0:T(8,128)(2,1)S(1)} %get-tuple-element.21), channel_id=1, source_target_pairs={{1,0},{2,1},{3,2},{4,3},{5,4},{6,5},{7,6},{8,7},{9,8},{10,9},{11,1... | collective-permute-start | bytes 147464 | tf_op jit(solution)/shard_map/ppermute | solution.py:278
  14.9 11.8 %copy-start.6 = (f32[3,3,2048]{2,1,0:T(4,128)S(1)}, f32[3,3,2048]{2,1,0:T(4,128)}, u32[]{:S(2)}) copy-start(f32[3,3,2048]{2,1,0:T(4,128)} %param.22) | copy-start | bytes 221188
  14.9 12.5 %collective-permute-start.2 = (bf16[48,512]{1,0:T(8,128)(2,1)S(1)}, bf16[48,512]{1,0:T(8,128)(2,1)S(1)}, u32[]{:S(2)}, u32[]{:S(2)}) collective-permute-start(bf16[48,512]{1,0:T(8,128)(2,1)S(1)} %get-tuple-element.22), channel_id=1, source_target_pairs={{0,1},{1,2},{2,3},{3,4},{4,5},{5,6},{6,7},{7,8},{8,9},{9,10},{10,1... | collective-permute-start | bytes 147464 | tf_op jit(solution)/shard_map/ppermute | solution.py:277
  27.4 0.6 copy-start.4
  27.4 0.6 copy-start.5
  51.0 33.8 %all-to-all-start = ((bf16[32,2,16,512]{3,2,1,0:T(8,128)(2,1)}), bf16[32,2,16,512]{3,2,1,0:T(8,128)(2,1)S(1)}, u32[]{:S(2)}, u32[]{:S(2)}) async-start(bf16[32,2,16,512]{3,2,1,0:T(8,128)(2,1)} %bitcast.23), calls=%async_computation | async-start | bytes 2097152 | tf_op jit(solution)/shard_map/all_to_all | solution.py:263
  84.7 10.0 %copy-start = (bf16[32,2,16,512]{3,2,1,0:T(8,128)(2,1)}, bf16[32,2,16,512]{3,2,1,0:T(8,128)(2,1)S(1)}, u32[]{:S(2)}) copy-start(bf16[32,2,16,512]{3,2,1,0:T(8,128)(2,1)S(1)} %all-to-all-done) | copy-start | bytes 3145732
  84.7 29.8 %all-to-all-start.2 = ((bf16[32,2,16,512]{3,2,1,0:T(8,128)(2,1)}), bf16[32,2,16,512]{3,2,1,0:T(8,128)(2,1)S(1)}, u32[]{:S(2)}, u32[]{:S(2)}) async-start(bf16[32,2,16,512]{3,2,1,0:T(8,128)(2,1)} %bitcast.26), calls=%async_computation.2 | async-start | bytes 2097152 | tf_op jit(solution)/shard_map/all_to_all | solution.py:263
  114.6 3.9 %copy-start.1 = (bf16[32,2,16,512]{3,2,1,0:T(8,128)(2,1)}, bf16[32,2,16,512]{3,2,1,0:T(8,128)(2,1)S(1)}, u32[]{:S(2)}) copy-start(bf16[32,2,16,512]{3,2,1,0:T(8,128)(2,1)S(1)} %all-to-all-done.2) | copy-start | bytes 3145732
  114.6 24.0 %all-to-all-start.1 = ((bf16[32,2,16,512]{3,2,1,0:T(8,128)(2,1)}), bf16[32,2,16,512]{3,2,1,0:T(8,128)(2,1)S(1)}, u32[]{:S(2)}, u32[]{:S(2)}) async-start(bf16[32,2,16,512]{3,2,1,0:T(8,128)(2,1)} %bitcast.25), calls=%async_computation.1 | async-start | bytes 2097152 | tf_op jit(solution)/shard_map/all_to_all | solution.py:263

commit v2 on v1

v2 whole, which is shorter than its diff:
```python
import functools

import jax
import jax.numpy as jnp
import numpy as np
from jax import lax
from jax.experimental import pallas as pl
from jax.experimental.pallas import tpu as pltpu
from jax.sharding import PartitionSpec as P

BF16 = jnp.bfloat16
F32 = jnp.float32
HEAD = 32
CHANS = 512
WIDE = 2048
CB = 512
VMEM_LIMIT = 56 * 2**20
SCALE_LOG2 = float(HEAD**-0.5 * np.log2(np.e))


def layer_norm(v):
    mean = jnp.mean(v, axis=-1, keepdims=True)
    cent = v - mean
    var = jnp.mean(cent * cent, axis=-1, keepdims=True)
    return (cent * lax.rsqrt(var + 1e-05)).astype(BF16)


def gelu(v):
    half = 0.5 * v
    return half + half * lax.erf(v * 0.7071067811865476)


def mm(a, b):
    return lax.dot_general(a, b, (((1,), (0,)), ((), ())), preferred_element_type=F32)


def mm_nt(a, b):
    return lax.dot_general(a, b, (((1,), (1,)), ((), ())), preferred_element_type=F32)


def permutation(dims, order):
    count = int(np.prod(dims))
    source = np.arange(count).reshape(dims).transpose(order).reshape(-1)
    matrix = np.zeros((count, count), np.float32)
    matrix[np.arange(count), source] = 1.0
    return jnp.asarray(matrix, BF16)


def whole(shape):
    zeros = (0,) * len(shape)
    return pl.BlockSpec(shape, lambda *_: zeros)


def params():
    return pltpu.CompilerParams(vmem_limit_bytes=VMEM_LIMIT)


def segment_max(scores):
    low = lax.broadcasted_iota(jnp.int32, (1, 128), 1) < 64
    found = []
    for at in range(0, scores.shape[1], 128):
        v = scores[:, at : at + 128]
        first = jnp.max(jnp.where(low, v, -jnp.inf), axis=-1, keepdims=True)
        second = jnp.max(jnp.where(low, -jnp.inf, v), axis=-1, keepdims=True)
        found.append(jnp.where(low, first, second))
    return jnp.concatenate(found, axis=1)


def attention(grouped, wqkv_ref, wo_ref, mask_ref, proj, context, emit):
    mask = mask_ref[...]
    for half in range(2):
        x = grouped[8 * half : 8 * half + 8].reshape(512, CHANS).astype(F32)
        proj[...] = mm(layer_norm(x), wqkv_ref[...]).astype(BF16)
        for g in range(8):
            rows = slice(64 * g, 64 * g + 64)
            for at in range(0, CHANS, 128):
                query = proj[rows, at : at + 128]
                keys = jnp.concatenate([proj[rows, CHANS + at : CHANS + at + 128]] * 4, axis=0) * mask
                values = jnp.concatenate([proj[rows, 2 * CHANS + at : 2 * CHANS + at + 128]] * 4, axis=0) * mask
                scores = mm_nt(query, keys)
                weights = jnp.exp2((scores - segment_max(scores)) * SCALE_LOG2).astype(BF16)
                both = mm(weights, jnp.concatenate([values, mask], axis=1))
                context[rows, at : at + 128] = (both[:, :128] / both[:, 128:]).astype(BF16)
        emit(half, x + mm(context[...], wo_ref[...]))


def grid_kernel(x_ref, wqkv_ref, wo_ref, turn_ref, mask_ref, out_ref, grouped, proj, context):
    for t in range(4):
        moved = mm(turn_ref[...], x_ref[16 * t : 16 * t + 16].reshape(256, CHANS))
        grouped[:, 16 * t : 16 * t + 16] = moved.astype(BF16).reshape(16, 16, CHANS)

    def emit(half, rows):
        grouped[8 * half : 8 * half + 8] = rows.astype(BF16).reshape(8, 64, CHANS)

    attention(grouped, wqkv_ref, wo_ref, mask_ref, proj, context, emit)
    for t in range(4):
        moved = mm(turn_ref[...], grouped[:, 16 * t : 16 * t + 16].reshape(256, CHANS))
        out_ref[16 * t : 16 * t + 16] = moved.astype(BF16).reshape(16, 16, CHANS)


def head_mask():
    return jnp.asarray(np.arange(256)[:, None] // 64 == np.arange(128)[None] // HEAD, BF16)


def attention_scratch():
    return [
        pltpu.VMEM((16, 64, CHANS), BF16),
        pltpu.VMEM((512, 3 * CHANS), BF16),
        pltpu.VMEM((512, CHANS), BF16),
    ]


def grid_attention(x, qkv, out_proj):
    return pl.pallas_call(
        grid_kernel,
        grid=(1,),
        in_specs=[
            whole((64, 16, CHANS)),
            whole((CHANS, 3 * CHANS)),
            whole((CHANS, CHANS)),
            whole((256, 256)),
            whole((256, 128)),
        ],
        out_specs=whole((64, 16, CHANS)),
        out_shape=jax.ShapeDtypeStruct((64, 16, CHANS), BF16),
        scratch_shapes=attention_scratch(),
        compiler_params=params(),
        cost_estimate=pl.CostEstimate(
            flops=8 * 1024 * CHANS * CHANS, bytes_accessed=4 * 2**20, transcendentals=2**20
        ),
        name="grid_attention",
    )(x, qkv, out_proj, permutation((16, 16), (1, 0)), head_mask())


def local_kernel(
    part, x_ref, prev_ref, next_ref, top_ref, bot_ref, left_ref, right_ref, we_ref, dw_ref, wp_ref, wqkv_ref, wo_ref,
    spread_ref, turn_ref, mask_ref, out_ref, normed, pad, rim, spatial, acc, grouped, proj, context,
):
    step = pl.program_id(0)

    @pl.when(step == 0)
    def _():
        for pair in range(4):
            moved = mm(spread_ref[...], x_ref[:, 2 * pair : 2 * pair + 2].reshape(256, CHANS))
            acc[256 * pair : 256 * pair + 256] = moved
            normed[128 + 256 * pair : 384 + 256 * pair] = layer_norm(moved)
        if part == 0:
            before, after = (top_ref[...], prev_ref[0, 0]), (next_ref[0, 0], next_ref[1, 0])
        else:
            before, after = (prev_ref[0, 0], prev_ref[1, 0]), (next_ref[1, 0], bot_ref[...])
        edges = jnp.concatenate([before[0], after[0], before[1], after[1]], axis=0)
        moved = layer_norm(mm(spread_ref[...], edges))
        normed[0:128] = moved[0:128]
        normed[1152:1280] = moved[128:256]
        normed[1280:1328] = layer_norm(left_ref[...].astype(F32))
        normed[1328:1376] = layer_norm(right_ref[...].astype(F32))

    for at in range(0, CB, 256):
        hidden = gelu(mm(normed[...], we_ref[:, at : at + 256])).astype(BF16)
        pad[:, 1:9, :, at : at + 256] = hidden[:1280].reshape(10, 8, 16, 256)
        rim[:, at : at + 256] = hidden[1280:].astype(F32)
    sub = lax.broadcasted_iota(jnp.int32, (8, CB), 0)
    for row in range(10):
        at = 8 * part + row
        last = pad[row, 8].astype(F32)
        first = pad[row, 1].astype(F32)
        west, east = [], []
        for b in range(2):
            turned = pltpu.roll(last[8 * b : 8 * b + 8], 1, 0)
            west.append(jnp.where(sub == 0, rim[at + 16 * b : at + 16 * b + 1], turned))
            turned = pltpu.roll(first[8 * b : 8 * b + 8], 7, 0)
            east.append(jnp.where(sub == 7, rim[at + 48 + 16 * b : at + 48 + 16 * b + 1], turned))
        pad[row, 0] = jnp.concatenate(west, axis=0).astype(BF16)
        pad[row, 9] = jnp.concatenate(east, axis=0).astype(BF16)

    for pair in range(4):
        for lane in range(0, CB, 128):
            lanes = slice(lane, lane + 128)
            taps = [dw_ref[t : t + 1, lanes].astype(BF16) for t in range(9)]
            for i in (2 * pair, 2 * pair + 1):
                tiles = [[pad[i + da, jj, :, lanes] for jj in range(10)] for da in range(3)]
                for j in range(8):
                    sums = [
                        tiles[da][j] * taps[3 * da]
                        + tiles[da][j + 1] * taps[3 * da + 1]
                        + tiles[da][j + 2] * taps[3 * da + 2]
                        for da in range(3)
                    ]
                    total = sums[0] + sums[1] + sums[2]
                    spatial[i, j, :, lanes] = gelu(total.astype(F32)).astype(BF16)
        rows = slice(256 * pair, 256 * pair + 256)
        acc[rows] += mm(spatial[2 * pair : 2 * pair + 2].reshape(256, CB), wp_ref[...])

    @pl.when(step == WIDE // CB - 1)
    def _():
        for pair in range(4):
            mixed = acc[256 * pair : 256 * pair + 256].astype(BF16)
            grouped[:, 16 * pair : 16 * pair + 16] = mm(turn_ref[...], mixed).astype(BF16).reshape(16, 16, CHANS)

        def emit(half, rows):
            rows = rows.reshape(4, 2, 8, 8, CHANS)
            for i in range(8):
                out_ref[i, :, half] = rows[:, :, i].reshape(4, 16, CHANS).astype(BF16)

        attention(grouped, wqkv_ref, wo_ref, mask_ref, proj, context, emit)


def local_part(part, field, rims, w_expand, dw, w_project, qkv, out_proj):
    rows = field.reshape(2, 16, 64, CHANS)

    def edge(at):
        return pl.BlockSpec((2, 1, 64, CHANS), lambda s: (0, at, 0, 0))

    return pl.pallas_call(
        functools.partial(local_kernel, part),
        grid=(WIDE // CB,),
        in_specs=[
            pl.BlockSpec((2, 8, 64, CHANS), lambda s: (0, part, 0, 0)),
            edge((15, 7)[part]),
            edge((8, 0)[part]),
            whole((64, CHANS)),
            whole((64, CHANS)),
            whole((48, CHANS)),
            whole((48, CHANS)),
            pl.BlockSpec((CHANS, CB), lambda s: (0, s)),
            pl.BlockSpec((9, CB), lambda s: (0, s)),
            pl.BlockSpec((CB, CHANS), lambda s: (s, 0)),
            whole((CHANS, 3 * CHANS)),
            whole((CHANS, CHANS)),
            whole((256, 256)),
            whole((256, 256)),
            whole((256, 128)),
        ],
        out_specs=whole((8, 4, 2, 16, CHANS)),
        out_shape=jax.ShapeDtypeStruct((8, 4, 2, 16, CHANS), BF16),
        scratch_shapes=[
            pltpu.VMEM((1376, CHANS), BF16),
            pltpu.VMEM((10, 10, 16, CB), BF16),
            pltpu.VMEM((96, CB), F32),
            pltpu.VMEM((8, 8, 16, CB), BF16),
            pltpu.VMEM((1024, CHANS), F32),
            *attention_scratch(),
        ],
        compiler_params=params(),
        cost_estimate=pl.CostEstimate(
            flops=4 * 1024 * CHANS * WIDE, bytes_accessed=8 * 2**20, transcendentals=2048 * WIDE
        ),
        name="local_part",
    )(
        rows, rows, rows, *rims, w_expand, dw, w_project, qkv, out_proj,
        permutation((2, 2, 8, 8), (1, 3, 0, 2)), permutation((16, 16), (1, 0)), head_mask(),
    )


def exchange(blocks, groups):
    return lax.all_to_all(blocks, ("row", "col"), 0, 0, axis_index_groups=groups, tiled=True)


def on_device(field, w_expand, dw_kernel, w_project, qkv_block, out_block, qkv_grid, out_grid):
    n_row, n_col = lax.axis_size("row"), lax.axis_size("col")
    down = [(i, i + 1) for i in range(n_row - 1)]
    up = [(i + 1, i) for i in range(n_row - 1)]
    top = lax.ppermute(field[31], "row", down)
    bottom = lax.ppermute(field[0], "row", up)
    fill = jnp.zeros((14, CHANS), BF16)

    def rim(column):
        return jnp.concatenate([top[column : column + 1], field[:, column], bottom[column : column + 1], fill], axis=0)

    left = lax.ppermute(rim(63), "col", [(i, i + 1) for i in range(n_col - 1)])
    right = lax.ppermute(rim(0), "col", [(i + 1, i) for i in range(n_col - 1)])
    rims = (top, bottom, left, right)
    dw = dw_kernel.reshape(9, WIDE)
    groups = [[32 * row + 4 * j + c for row in range(n_row) for j in range(8)] for c in range(4)]
    homes = []
    for part in range(2):
        blocked = local_part(part, field, rims, w_expand, dw, w_project, qkv_block, out_block)
        gathered = exchange(blocked.reshape(32, 2, 16, CHANS), groups).reshape(64, 16, CHANS)
        attended = grid_attention(gathered, qkv_grid, out_grid)
        homes.append(exchange(attended.reshape(32, 2, 16, CHANS), groups))
    home = jnp.stack(homes).reshape(2, 8, 4, 2, 16, CHANS)
    return home.transpose(3, 0, 1, 2, 4, 5).reshape(32, 64, CHANS)


def solution(mesh):
    placed = (P("row", "col", None), P(), P(), P(), P(), P(), P(), P())
    return jax.shard_map(
        on_device, mesh=mesh, in_specs=placed, out_specs=P("row", "col", None), check_vma=False
    )
```

time: 166 us -> 163 us (0.982)
  Pallas kernels: 78.2 us -> 67.8 us
  starting transfers between devices: 35.1 us -> 42.9 us
    pallas_call x8 -> x4, Pallas kernels: 78.2 us -> 67.8 us  [the longest x2 49.4 us: local_part(): pl.pallas_call(functools.partial(local_kernel, part), grid=(WIDE // CB,),...]
    all_to_all x3, starting transfers between devices: 24.8 us -> 32.7 us  [exchange(): lax.all_to_all(blocks, ('row', 'col'), 0, 0, axis_index_groups=groups, ti...]
  transfers between devices with their start and end apart: 7 -> 7, of which waited for: 2 -> 3; matrix products, arithmetic and copies ran while one was open for 1% -> 2% of each run, Pallas kernels for 34% -> 27%
where the time goes in v2:
time: 163 us
  Pallas kernels  67.8 us (42%)
  starting transfers between devices  42.9 us (26%)
  blocking collectives  23.9 us (15%)
  waiting for transfers between devices  21.6 us (13%)
  local copies, waits for them, and re-layouts  5.85 us (4%)
    pallas_call x2, Pallas kernels, local_part(): pl.pallas_call(functools.partial(local_kernel, part), grid=(WIDE // CB,),...  49.4 us
    all_to_all x3, starting transfers between devices, exchange(): lax.all_to_all(blocks, ('row', 'col'), 0, 0, axis_index_groups=groups, ti...  32.7 us
    all_to_all x1, blocking collectives, exchange(): lax.all_to_all(blocks, ('row', 'col'), 0, 0, axis_index_groups=groups, ti...  23.9 us
    all_to_all x3, waiting for transfers between devices, exchange(): lax.all_to_all(blocks, ('row', 'col'), 0, 0, axis_index_groups=groups, ti...  21.4 us
    pallas_call x2, Pallas kernels, grid_attention(): pl.pallas_call(grid_kernel, grid=(1,), in_specs=[whole((64, 16, CHANS)),...  18.4 us
    ppermute x1, starting transfers between devices, on_device(): left = lax.ppermute(rim(63), 'col', [(i, i + 1) for i in range(n_col - 1)])  4.55 us
  transfers between devices with their start and end apart: 7, of which 3 were waited for; matrix products, arithmetic and copies ran while one was open for 2% of the time, Pallas kernels for 27%

profile of v2, /device:TPU:0, one launch (start us, length us, event | category | flops | bytes accessed | tf_op | source)
XLA Modules:
  0.0 162.5 jit_solution(13082901125090887421)
XLA Ops:
  0.0 0.9 slice_bitcast_fusion
  0.9 1.3 collective-permute-start.1
  2.2 3.0 %collective-permute-start = (bf16[64,512]{1,0:T(8,128)(2,1)S(1)}, bf16[64,512]{1,0:T(8,128)(2,1)S(1)}, u32[]{:S(2)}, u32[]{:S(2)}) collective-permute-start(bf16[64,512]{1,0:T(8,128)(2,1)S(1)} %get-tuple-element.8), channel_id=1, source_target_pairs={{0,32},{32,64},{64,96},{1,33},{33,65},{65,97},{2,34},{34,66},{66,9... | collective-permute-start | bytes 196616 | tf_op jit(solution)/shard_map/ppermute | solution.py:263
  5.2 1.1 fusion
  6.4 0.1 pad.9.clone
  6.5 0.0 collective-permute-done.1.bot_ref
  6.5 0.0 copy-start.2
  6.5 0.0 collective-permute-done.top_ref
  6.5 0.0 copy-start.3
  6.5 0.1 maximum_maximum_fusion.1
  6.6 1.3 collective-permute-start.3
  7.9 4.5 %collective-permute-start.2 = (bf16[48,512]{1,0:T(8,128)(2,1)S(1)}, bf16[48,512]{1,0:T(8,128)(2,1)S(1)}, u32[]{:S(2)}, u32[]{:S(2)}) collective-permute-start(bf16[48,512]{1,0:T(8,128)(2,1)S(1)} %get-tuple-element.14), channel_id=1, source_target_pairs={{0,1},{1,2},{2,3},{3,4},{4,5},{5,6},{6,7},{7,8},{8,9},{9,10},{10,1... | collective-permute-start | bytes 147464 | tf_op jit(solution)/shard_map/ppermute | solution.py:270
  12.5 1.6 reshape.34.dw_ref
  14.1 0.0 collective-permute-done.3.right_ref
  14.1 0.0 copy-start.4
  14.1 0.1 collective-permute-done.2.left_ref
  14.2 0.0 copy-start.5
  14.2 0.0 copy-done.2
  14.2 0.0 copy-done.3
  14.2 0.5 copy-done.4
  14.7 0.1 copy-done.5
  14.8 24.7 %local_part.3 = bf16[8,4,2,16,512]{4,3,2,1,0:T(8,128)(2,1)} custom-call(bf16[2,16,64,512]{3,2,1,0:T(8,128)(2,1)} %bitcast.28, bf16[2,16,64,512]{3,2,1,0:T(8,128)(2,1)} %bitcast.29, bf16[2,16,64,512]{3,2,1,0:T(8,128)(2,1)} %bitcast.30, bf16[64,512]{1,0:T(8,128)(2,1)} %copy-done.3, bf16[64,512]{1,0:T(8,128)(2,1)} %copy-done.2, bf16[48,512]{1,0:T(8,128)(2,1)} %copy-done.5, ...), custom_call_target="tpu_custom_call" | custom-call | flops 4294967296 | bytes 8388608 | tf_op jit(solution)/shard_map/local_part/pallas_call | solution.py:214
  39.5 19.0 %all-to-all-start.2 = ((bf16[32,2,16,512]{3,2,1,0:T(8,128)(2,1)}), bf16[32,2,16,512]{3,2,1,0:T(8,128)(2,1)S(1)}, u32[]{:S(2)}, u32[]{:S(2)}) async-start(bf16[32,2,16,512]{3,2,1,0:T(8,128)(2,1)} %bitcast.26), calls=%async_computation.2 | async-start | bytes 2097152 | tf_op jit(solution)/shard_map/all_to_all | solution.py:256
  58.5 24.7 %local_part.2 = bf16[8,4,2,16,512]{4,3,2,1,0:T(8,128)(2,1)} custom-call(bf16[2,16,64,512]{3,2,1,0:T(8,128)(2,1)} %bitcast.31, bf16[2,16,64,512]{3,2,1,0:T(8,128)(2,1)} %bitcast.32, bf16[2,16,64,512]{3,2,1,0:T(8,128)(2,1)} %bitcast.33, bf16[64,512]{1,0:T(8,128)(2,1)} %copy-done.3, bf16[64,512]{1,0:T(8,128)(2,1)} %copy-done.2, bf16[48,512]{1,0:T(8,128)(2,1)} %copy-done.5, ...), custom_call_target="tpu_custom_call" | custom-call | flops 4294967296 | bytes 8388608 | tf_op jit(solution)/shard_map/local_part/pallas_call | solution.py:214
  83.2 0.0 all-to-all-done.2
  83.2 0.0 copy-start
  83.2 9.9 %all-to-all-start = ((bf16[32,2,16,512]{3,2,1,0:T(8,128)(2,1)}), bf16[32,2,16,512]{3,2,1,0:T(8,128)(2,1)S(1)}, u32[]{:S(2)}, u32[]{:S(2)}) async-start(bf16[32,2,16,512]{3,2,1,0:T(8,128)(2,1)} %bitcast.24), calls=%async_computation | async-start | bytes 2097152 | tf_op jit(solution)/shard_map/all_to_all | solution.py:256
  93.1 0.0 copy-done
  93.1 9.2 %grid_attention.3 = bf16[64,16,512]{2,1,0:T(8,128)(2,1)} custom-call(bf16[64,16,512]{2,1,0:T(8,128)(2,1)} %bitcast.22, bf16[512,1536]{1,0:T(8,128)(2,1)} %wqkv_ref.7, bf16[512,512]{1,0:T(8,128)(2,1)} %wo_ref.7, bf16[256,256]{1,0:T(8,128)(2,1)} %constant.9.clone.turn_ref, bf16[256,128]{1,0:T(8,128)(2,1)} %constant.10.clone.mask_ref), custom_call_target="tpu_custom_call" | custom-call | flops 2147483648 | bytes 4194304 | tf_op jit(solution)/shard_map/grid_attention/pallas_call | solution.py:114
  102.3 10.6 %all-to-all-done = bf16[32,2,16,512]{3,2,1,0:T(8,128)(2,1)S(1)} async-done(((bf16[32,2,16,512]{3,2,1,0:T(8,128)(2,1)}), bf16[32,2,16,512]{3,2,1,0:T(8,128)(2,1)S(1)}, u32[]{:S(2)}, u32[]{:S(2)}) %all-to-all-start) | async-done | bytes 1048608 | tf_op jit(solution)/shard_map/all_to_all | solution.py:256
  112.9 0.0 copy-start.1
  112.9 3.9 %all-to-all-start.3 = ((bf16[32,2,16,512]{3,2,1,0:T(8,128)(2,1)}), bf16[32,2,16,512]{3,2,1,0:T(8,128)(2,1)S(1)}, u32[]{:S(2)}, u32[]{:S(2)}) async-start(bf16[32,2,16,512]{3,2,1,0:T(8,128)(2,1)} %bitcast.25), calls=%async_computation.3 | async-start | bytes 2097152 | tf_op jit(solution)/shard_map/all_to_all | solution.py:256
  116.8 0.0 copy-done.1
  116.8 9.2 %grid_attention.2 = bf16[64,16,512]{2,1,0:T(8,128)(2,1)} custom-call(bf16[64,16,512]{2,1,0:T(8,128)(2,1)} %bitcast.23, bf16[512,1536]{1,0:T(8,128)(2,1)} %wqkv_ref.7, bf16[512,512]{1,0:T(8,128)(2,1)} %wo_ref.7, bf16[256,256]{1,0:T(8,128)(2,1)} %constant.9.clone.turn_ref, bf16[256,128]{1,0:T(8,128)(2,1)} %constant.10.clone.mask_ref), custom_call_target="tpu_custom_call" | custom-call | flops 2147483648 | bytes 4194304 | tf_op jit(solution)/shard_map/grid_attention/pallas_call | solution.py:114
  126.0 10.8 %all-to-all-done.3 = bf16[32,2,16,512]{3,2,1,0:T(8,128)(2,1)S(1)} async-done(((bf16[32,2,16,512]{3,2,1,0:T(8,128)(2,1)}), bf16[32,2,16,512]{3,2,1,0:T(8,128)(2,1)S(1)}, u32[]{:S(2)}, u32[]{:S(2)}) %all-to-all-start.3) | async-done | bytes 1048608 | tf_op jit(solution)/shard_map/all_to_all | solution.py:256
  136.9 23.9 %all_to_all.20 = bf16[32,2,16,512]{3,2,1,0:T(8,128)(2,1)S(1)} all-to-all(bf16[32,2,16,512]{3,2,1,0:T(8,128)(2,1)} %bitcast.27), channel_id=1, replica_groups={{0,4,8,12,16,20,24,28,32,36,40,44,48,52,56,60,64,68,72,76,80,84,88,92,9..., dimensions={0} | all-to-all | bytes 2097152 | tf_op jit(solution)/shard_map/all_to_all | solution.py:256
  160.8 0.2 pad_maximum_fusion
  161.0 1.5 copy.23
  (4 shorter events, 0.0 us)
Async XLA Ops:
  0.9 5.6 %collective-permute-start.1 = (bf16[64,512]{1,0:T(8,128)(2,1)S(1)}, bf16[64,512]{1,0:T(8,128)(2,1)S(1)}, u32[]{:S(2)}, u32[]{:S(2)}) collective-permute-start(bf16[64,512]{1,0:T(8,128)(2,1)S(1)} %get-tuple-element.7), channel_id=1, source_target_pairs={{32,0},{64,32},{96,64},{33,1},{65,33},{97,65},{34,2},{66,34},{98,6... | collective-permute-start | bytes 196616 | tf_op jit(solution)/shard_map/ppermute | solution.py:264
  2.2 4.3 %collective-permute-start = (bf16[64,512]{1,0:T(8,128)(2,1)S(1)}, bf16[64,512]{1,0:T(8,128)(2,1)S(1)}, u32[]{:S(2)}, u32[]{:S(2)}) collective-permute-start(bf16[64,512]{1,0:T(8,128)(2,1)S(1)} %get-tuple-element.8), channel_id=1, source_target_pairs={{0,32},{32,64},{64,96},{1,33},{33,65},{65,97},{2,34},{34,66},{66,9... | collective-permute-start | bytes 196616 | tf_op jit(solution)/shard_map/ppermute | solution.py:263
  6.5 7.7 %copy-start.2 = (bf16[64,512]{1,0:T(8,128)(2,1)}, bf16[64,512]{1,0:T(8,128)(2,1)S(1)}, u32[]{:S(2)}) copy-start(bf16[64,512]{1,0:T(8,128)(2,1)S(1)} %collective-permute-done.1.bot_ref) | copy-start | bytes 196612
  6.5 7.7 %copy-start.3 = (bf16[64,512]{1,0:T(8,128)(2,1)}, bf16[64,512]{1,0:T(8,128)(2,1)S(1)}, u32[]{:S(2)}) copy-start(bf16[64,512]{1,0:T(8,128)(2,1)S(1)} %collective-permute-done.top_ref) | copy-start | bytes 196612
  6.6 7.4 %collective-permute-start.3 = (bf16[48,512]{1,0:T(8,128)(2,1)S(1)}, bf16[48,512]{1,0:T(8,128)(2,1)S(1)}, u32[]{:S(2)}, u32[]{:S(2)}) collective-permute-start(bf16[48,512]{1,0:T(8,128)(2,1)S(1)} %get-tuple-element.13), channel_id=1, source_target_pairs={{1,0},{2,1},{3,2},{4,3},{5,4},{6,5},{7,6},{8,7},{9,8},{10,9},{11,1... | collective-permute-start | bytes 147464 | tf_op jit(solution)/shard_map/ppermute | solution.py:271
  7.9 6.3 %collective-permute-start.2 = (bf16[48,512]{1,0:T(8,128)(2,1)S(1)}, bf16[48,512]{1,0:T(8,128)(2,1)S(1)}, u32[]{:S(2)}, u32[]{:S(2)}) collective-permute-start(bf16[48,512]{1,0:T(8,128)(2,1)S(1)} %get-tuple-element.14), channel_id=1, source_target_pairs={{0,1},{1,2},{2,3},{3,4},{4,5},{5,6},{6,7},{7,8},{8,9},{9,10},{10,1... | collective-permute-start | bytes 147464 | tf_op jit(solution)/shard_map/ppermute | solution.py:270
  14.1 0.6 copy-start.4
  14.2 0.6 copy-start.5
  39.5 43.7 %all-to-all-start.2 = ((bf16[32,2,16,512]{3,2,1,0:T(8,128)(2,1)}), bf16[32,2,16,512]{3,2,1,0:T(8,128)(2,1)S(1)}, u32[]{:S(2)}, u32[]{:S(2)}) async-start(bf16[32,2,16,512]{3,2,1,0:T(8,128)(2,1)} %bitcast.26), calls=%async_computation.2 | async-start | bytes 2097152 | tf_op jit(solution)/shard_map/all_to_all | solution.py:256
  83.2 9.9 %copy-start = (bf16[32,2,16,512]{3,2,1,0:T(8,128)(2,1)}, bf16[32,2,16,512]{3,2,1,0:T(8,128)(2,1)S(1)}, u32[]{:S(2)}) copy-start(bf16[32,2,16,512]{3,2,1,0:T(8,128)(2,1)S(1)} %all-to-all-done.2) | copy-start | bytes 3145732
  83.2 29.7 %all-to-all-start = ((bf16[32,2,16,512]{3,2,1,0:T(8,128)(2,1)}), bf16[32,2,16,512]{3,2,1,0:T(8,128)(2,1)S(1)}, u32[]{:S(2)}, u32[]{:S(2)}) async-start(bf16[32,2,16,512]{3,2,1,0:T(8,128)(2,1)} %bitcast.24), calls=%async_computation | async-start | bytes 2097152 | tf_op jit(solution)/shard_map/all_to_all | solution.py:256
  112.9 3.9 %copy-start.1 = (bf16[32,2,16,512]{3,2,1,0:T(8,128)(2,1)}, bf16[32,2,16,512]{3,2,1,0:T(8,128)(2,1)S(1)}, u32[]{:S(2)}) copy-start(bf16[32,2,16,512]{3,2,1,0:T(8,128)(2,1)S(1)} %all-to-all-done) | copy-start | bytes 3145732
  112.9 24.0 %all-to-all-start.3 = ((bf16[32,2,16,512]{3,2,1,0:T(8,128)(2,1)}), bf16[32,2,16,512]{3,2,1,0:T(8,128)(2,1)S(1)}, u32[]{:S(2)}, u32[]{:S(2)}) async-start(bf16[32,2,16,512]{3,2,1,0:T(8,128)(2,1)} %bitcast.25), calls=%async_computation.3 | async-start | bytes 2097152 | tf_op jit(solution)/shard_map/all_to_all | solution.py:256

commit v3 on v2

--- a/solution.py
+++ b/solution.py
@@ -13,7 +13,7 @@
 HEAD = 32
 CHANS = 512
 WIDE = 2048
-CB = 512
+CB = 1024
 VMEM_LIMIT = 56 * 2**20
 SCALE_LOG2 = float(HEAD**-0.5 * np.log2(np.e))
 
@@ -84,7 +84,8 @@
         emit(half, x + mm(context[...], wo_ref[...]))
 
 
-def grid_kernel(x_ref, wqkv_ref, wo_ref, turn_ref, mask_ref, out_ref, grouped, proj, context):
+def grid_kernel(x_ref, wqkv_ref, wo_ref, turn_ref, mask_ref, *rest):
+    out_ref, grouped, proj, context = rest[-4:]
     for t in range(4):
         moved = mm(turn_ref[...], x_ref[16 * t : 16 * t + 16].reshape(256, CHANS))
         grouped[:, 16 * t : 16 * t + 16] = moved.astype(BF16).reshape(16, 16, CHANS)
@@ -95,7 +96,7 @@
     attention(grouped, wqkv_ref, wo_ref, mask_ref, proj, context, emit)
     for t in range(4):
         moved = mm(turn_ref[...], grouped[:, 16 * t : 16 * t + 16].reshape(256, CHANS))
-        out_ref[16 * t : 16 * t + 16] = moved.astype(BF16).reshape(16, 16, CHANS)
+        out_ref[8 * t : 8 * t + 8, 0] = moved.astype(BF16).reshape(8, 2, 16, CHANS)
 
 
 def head_mask():
@@ -110,7 +111,9 @@
     ]
 
 
-def grid_attention(x, qkv, out_proj):
+def grid_attention(part, x, qkv, out_proj, earlier):
+    shape = (32, 2, 2, 16, CHANS)
+    kept = [] if earlier is None else [earlier]
     return pl.pallas_call(
         grid_kernel,
         grid=(1,),
@@ -120,16 +123,18 @@
             whole((CHANS, CHANS)),
             whole((256, 256)),
             whole((256, 128)),
+            *[pl.BlockSpec(memory_space=pl.ANY) for _ in kept],
         ],
-        out_specs=whole((64, 16, CHANS)),
-        out_shape=jax.ShapeDtypeStruct((64, 16, CHANS), BF16),
+        out_specs=pl.BlockSpec((32, 1, 2, 16, CHANS), lambda s: (0, part, 0, 0, 0)),
+        out_shape=jax.ShapeDtypeStruct(shape, BF16),
         scratch_shapes=attention_scratch(),
+        input_output_aliases={5: 0} if kept else {},
         compiler_params=params(),
         cost_estimate=pl.CostEstimate(
             flops=8 * 1024 * CHANS * CHANS, bytes_accessed=4 * 2**20, transcendentals=2**20
         ),
         name="grid_attention",
-    )(x, qkv, out_proj, permutation((16, 16), (1, 0)), head_mask())
+    )(x, qkv, out_proj, permutation((16, 16), (1, 0)), head_mask(), *kept)
 
 
 def local_kernel(
@@ -173,21 +178,16 @@
         pad[row, 0] = jnp.concatenate(west, axis=0).astype(BF16)
         pad[row, 9] = jnp.concatenate(east, axis=0).astype(BF16)
 
+    taps = [[jnp.broadcast_to(dw_ref[a, b : b + 1].astype(BF16), (16, CB)) for b in range(3)] for a in range(3)]
     for pair in range(4):
-        for lane in range(0, CB, 128):
-            lanes = slice(lane, lane + 128)
-            taps = [dw_ref[t : t + 1, lanes].astype(BF16) for t in range(9)]
-            for i in (2 * pair, 2 * pair + 1):
-                tiles = [[pad[i + da, jj, :, lanes] for jj in range(10)] for da in range(3)]
-                for j in range(8):
-                    sums = [
-                        tiles[da][j] * taps[3 * da]
-                        + tiles[da][j + 1] * taps[3 * da + 1]
-                        + tiles[da][j + 2] * taps[3 * da + 2]
-                        for da in range(3)
-                    ]
-                    total = sums[0] + sums[1] + sums[2]
-                    spatial[i, j, :, lanes] = gelu(total.astype(F32)).astype(BF16)
+        for i in (2 * pair, 2 * pair + 1):
+            for j in range(8):
+                sums = [
+                    pad[i + a, j] * taps[a][0] + pad[i + a, j + 1] * taps[a][1] + pad[i + a, j + 2] * taps[a][2]
+                    for a in range(3)
+                ]
+                total = sums[0] + sums[1] + sums[2]
+                spatial[i, j] = gelu(total.astype(F32)).astype(BF16)
         rows = slice(256 * pair, 256 * pair + 256)
         acc[rows] += mm(spatial[2 * pair : 2 * pair + 2].reshape(256, CB), wp_ref[...])
 
@@ -205,7 +205,7 @@
         attention(grouped, wqkv_ref, wo_ref, mask_ref, proj, context, emit)
 
 
-def local_part(part, field, rims, w_expand, dw, w_project, qkv, out_proj):
+def local_part(part, field, rims, w_expand, dw_kernel, w_project, qkv, out_proj):
     rows = field.reshape(2, 16, 64, CHANS)
 
     def edge(at):
@@ -223,7 +223,7 @@
             whole((48, CHANS)),
             whole((48, CHANS)),
             pl.BlockSpec((CHANS, CB), lambda s: (0, s)),
-            pl.BlockSpec((9, CB), lambda s: (0, s)),
+            pl.BlockSpec((3, 3, CB), lambda s: (0, 0, s)),
             pl.BlockSpec((CB, CHANS), lambda s: (s, 0)),
             whole((CHANS, 3 * CHANS)),
             whole((CHANS, CHANS)),
@@ -247,7 +247,7 @@
         ),
         name="local_part",
     )(
-        rows, rows, rows, *rims, w_expand, dw, w_project, qkv, out_proj,
+        rows, rows, rows, *rims, w_expand, dw_kernel, w_project, qkv, out_proj,
         permutation((2, 2, 8, 8), (1, 3, 0, 2)), permutation((16, 16), (1, 0)), head_mask(),
     )
 
@@ -270,16 +270,16 @@
     left = lax.ppermute(rim(63), "col", [(i, i + 1) for i in range(n_col - 1)])
     right = lax.ppermute(rim(0), "col", [(i + 1, i) for i in range(n_col - 1)])
     rims = (top, bottom, left, right)
-    dw = dw_kernel.reshape(9, WIDE)
     groups = [[32 * row + 4 * j + c for row in range(n_row) for j in range(8)] for c in range(4)]
-    homes = []
+    gathered = []
     for part in range(2):
-        blocked = local_part(part, field, rims, w_expand, dw, w_project, qkv_block, out_block)
-        gathered = exchange(blocked.reshape(32, 2, 16, CHANS), groups).reshape(64, 16, CHANS)
-        attended = grid_attention(gathered, qkv_grid, out_grid)
-        homes.append(exchange(attended.reshape(32, 2, 16, CHANS), groups))
-    home = jnp.stack(homes).reshape(2, 8, 4, 2, 16, CHANS)
-    return home.transpose(3, 0, 1, 2, 4, 5).reshape(32, 64, CHANS)
+        blocked = local_part(part, field, rims, w_expand, dw_kernel, w_project, qkv_block, out_block)
+        gathered.append(exchange(blocked.reshape(32, 2, 16, CHANS), groups).reshape(64, 16, CHANS))
+    attended = None
+    for part in range(2):
+        attended = grid_attention(part, gathered[part], qkv_grid, out_grid, attended)
+    home = exchange(attended, groups).reshape(8, 4, 2, 2, 16, CHANS)
+    return home.transpose(3, 2, 0, 1, 4, 5).reshape(32, 64, CHANS)
 
 
 def solution(mesh):

time: 163 us -> 150 us (0.920)
  blocking collectives: 23.9 us -> 35.3 us
  Pallas kernels: 67.8 us -> 56.9 us
  waiting for transfers between devices: 21.6 us -> 12.9 us
  starting transfers between devices: 42.9 us -> 38.5 us
    all_to_all x1, blocking collectives: 23.9 us -> 35.3 us  [exchange(): lax.all_to_all(blocks, ('row', 'col'), 0, 0, axis_index_groups=groups, ti...]
    pallas_call x2, Pallas kernels: 49.4 us -> 38.6 us  [local_part(): pl.pallas_call(functools.partial(local_kernel, part), grid=(WIDE // CB,),...]
    all_to_all x3 -> x2, waiting for transfers between devices: 21.4 us -> 11.2 us  [exchange(): lax.all_to_all(blocks, ('row', 'col'), 0, 0, axis_index_groups=groups, ti...]
    all_to_all x3 -> x2, starting transfers between devices: 32.7 us -> 28.3 us  [exchange(): lax.all_to_all(blocks, ('row', 'col'), 0, 0, axis_index_groups=groups, ti...]
  transfers between devices with their start and end apart: 7 -> 6, of which waited for: 3 -> 4; matrix products, arithmetic and copies ran while one was open for 2% -> 1% of each run, Pallas kernels for 27% -> 19%
where the time goes in v3:
time: 150 us; the launch traced here: 149 us
  Pallas kernels  56.9 us (38%)
  starting transfers between devices  38.5 us (26%)
  blocking collectives  35.3 us (24%)
  waiting for transfers between devices  12.9 us (9%)
  local copies, waits for them, and re-layouts  5.24 us (3%)
    pallas_call x2, Pallas kernels, local_part(): pl.pallas_call(functools.partial(local_kernel, part), grid=(WIDE // CB,),...  38.6 us
    all_to_all x1, blocking collectives, exchange(): lax.all_to_all(blocks, ('row', 'col'), 0, 0, axis_index_groups=groups, ti...  35.3 us
    all_to_all x2, starting transfers between devices, exchange(): lax.all_to_all(blocks, ('row', 'col'), 0, 0, axis_index_groups=groups, ti...  28.3 us
    pallas_call x2, Pallas kernels, grid_attention(): pl.pallas_call(grid_kernel, grid=(1,), in_specs=[whole((64, 16, CHANS)),...  18.3 us
    all_to_all x2, waiting for transfers between devices, exchange(): lax.all_to_all(blocks, ('row', 'col'), 0, 0, axis_index_groups=groups, ti...  11.2 us
    ppermute x1, starting transfers between devices, on_device(): left = lax.ppermute(rim(63), 'col', [(i, i + 1) for i in range(n_col - 1)])  4.55 us
    ppermute x1, starting transfers between devices, on_device(): top = lax.ppermute(field[31], 'row', down)  3.03 us
  transfers between devices with their start and end apart: 6, of which 4 were waited for; matrix products, arithmetic and copies ran while one was open for 1% of the time, Pallas kernels for 19%

profile of v3, /device:TPU:0, one launch (start us, length us, event | category | flops | bytes accessed | tf_op | source)
XLA Modules:
  0.0 149.0 jit_solution(5166401230861584897)
XLA Ops:
  0.0 0.9 slice_bitcast_fusion
  0.9 1.3 collective-permute-start.1
  2.2 3.0 %collective-permute-start = (bf16[64,512]{1,0:T(8,128)(2,1)S(1)}, bf16[64,512]{1,0:T(8,128)(2,1)S(1)}, u32[]{:S(2)}, u32[]{:S(2)}) collective-permute-start(bf16[64,512]{1,0:T(8,128)(2,1)S(1)} %get-tuple-element.8), channel_id=1, source_target_pairs={{0,32},{32,64},{64,96},{1,33},{33,65},{65,97},{2,34},{34,66},{66,9... | collective-permute-start | bytes 196616 | tf_op jit(solution)/shard_map/ppermute | solution.py:263
  5.2 1.1 fusion
  6.4 0.1 pad.7.clone
  6.5 0.0 collective-permute-done.1.bot_ref
  6.5 0.0 copy-start.2
  6.5 0.0 collective-permute-done.top_ref
  6.5 0.0 copy-start.3
  6.5 0.1 maximum_maximum_fusion.1
  6.6 1.3 collective-permute-start.3
  7.9 4.5 %collective-permute-start.2 = (bf16[48,512]{1,0:T(8,128)(2,1)S(1)}, bf16[48,512]{1,0:T(8,128)(2,1)S(1)}, u32[]{:S(2)}, u32[]{:S(2)}) collective-permute-start(bf16[48,512]{1,0:T(8,128)(2,1)S(1)} %get-tuple-element.14), channel_id=1, source_target_pairs={{0,1},{1,2},{2,3},{3,4},{4,5},{5,6},{6,7},{7,8},{8,9},{9,10},{10,1... | collective-permute-start | bytes 147464 | tf_op jit(solution)/shard_map/ppermute | solution.py:270
  12.5 0.1 collective-permute-done.3.right_ref
  12.6 0.0 copy-start.4
  12.6 1.6 %collective-permute-done.2.left_ref = bf16[48,512]{1,0:T(8,128)(2,1)S(1)} collective-permute-done((bf16[48,512]{1,0:T(8,128)(2,1)S(1)}, bf16[48,512]{1,0:T(8,128)(2,1)S(1)}, u32[]{:S(2)}, u32[]{:S(2)}) %collective-permute-start.2) | collective-permute-done | bytes 49184 | tf_op jit(solution)/shard_map/ppermute | solution.py:270
  14.2 0.0 copy-start.5
  14.2 0.0 copy-done.2
  14.2 0.0 copy-done.3
  14.2 0.0 copy-done.4
  14.2 0.6 copy-done.5
  14.8 19.2 %local_part.3 = bf16[8,4,2,16,512]{4,3,2,1,0:T(8,128)(2,1)} custom-call(bf16[2,16,64,512]{3,2,1,0:T(8,128)(2,1)} %bitcast.22, bf16[2,16,64,512]{3,2,1,0:T(8,128)(2,1)} %bitcast.23, bf16[2,16,64,512]{3,2,1,0:T(8,128)(2,1)} %bitcast.24, bf16[64,512]{1,0:T(8,128)(2,1)} %copy-done.3, bf16[64,512]{1,0:T(8,128)(2,1)} %copy-done.2, bf16[48,512]{1,0:T(8,128)(2,1)} %copy-done.5, ...), custom_call_target="tpu_custom_call" | custom-call | flops 4294967296 | bytes 8388608 | tf_op jit(solution)/shard_map/local_part/pallas_call | solution.py:214
  34.1 19.0 %all-to-all-start.1 = ((bf16[32,2,16,512]{3,2,1,0:T(8,128)(2,1)}), bf16[32,2,16,512]{3,2,1,0:T(8,128)(2,1)S(1)}, u32[]{:S(2)}, u32[]{:S(2)}) async-start(bf16[32,2,16,512]{3,2,1,0:T(8,128)(2,1)} %bitcast.21), calls=%async_computation.1 | async-start | bytes 2097152 | tf_op jit(solution)/shard_map/all_to_all | solution.py:256
  53.0 19.3 %local_part.2 = bf16[8,4,2,16,512]{4,3,2,1,0:T(8,128)(2,1)} custom-call(bf16[2,16,64,512]{3,2,1,0:T(8,128)(2,1)} %bitcast.25, bf16[2,16,64,512]{3,2,1,0:T(8,128)(2,1)} %bitcast.26, bf16[2,16,64,512]{3,2,1,0:T(8,128)(2,1)} %bitcast.27, bf16[64,512]{1,0:T(8,128)(2,1)} %copy-done.3, bf16[64,512]{1,0:T(8,128)(2,1)} %copy-done.2, bf16[48,512]{1,0:T(8,128)(2,1)} %copy-done.5, ...), custom_call_target="tpu_custom_call" | custom-call | flops 4294967296 | bytes 8388608 | tf_op jit(solution)/shard_map/local_part/pallas_call | solution.py:214
  72.4 0.5 all-to-all-done.1
  72.9 0.0 copy-start
  72.9 9.3 %all-to-all-start = ((bf16[32,2,16,512]{3,2,1,0:T(8,128)(2,1)}), bf16[32,2,16,512]{3,2,1,0:T(8,128)(2,1)S(1)}, u32[]{:S(2)}, u32[]{:S(2)}) async-start(bf16[32,2,16,512]{3,2,1,0:T(8,128)(2,1)} %bitcast.19), calls=%async_computation | async-start | bytes 2097152 | tf_op jit(solution)/shard_map/all_to_all | solution.py:256
  82.2 0.0 copy-done
  82.3 9.2 %grid_attention.2.rest_0_ = bf16[32,2,2,16,512]{4,3,2,1,0:T(8,128)(2,1)} custom-call(bf16[64,16,512]{2,1,0:T(8,128)(2,1)} %bitcast.18, bf16[512,1536]{1,0:T(8,128)(2,1)} %wqkv_ref.7, bf16[512,512]{1,0:T(8,128)(2,1)} %wo_ref.7, bf16[256,256]{1,0:T(8,128)(2,1)} %constant.9.clone.turn_ref, bf16[256,128]{1,0:T(8,128)(2,1)} %constant.10.clone.mask_ref), custom_call_target="tpu_custom_call" | custom-call | flops 2147483648 | bytes 4194304 | tf_op jit(solution)/shard_map/grid_attention/pallas_call | solution.py:117
  91.4 10.6 %all-to-all-done = bf16[32,2,16,512]{3,2,1,0:T(8,128)(2,1)S(1)} async-done(((bf16[32,2,16,512]{3,2,1,0:T(8,128)(2,1)}), bf16[32,2,16,512]{3,2,1,0:T(8,128)(2,1)S(1)}, u32[]{:S(2)}, u32[]{:S(2)}) %all-to-all-start) | async-done | bytes 1048608 | tf_op jit(solution)/shard_map/all_to_all | solution.py:256
  102.0 0.0 copy-start.1
  102.0 1.0 copy-done.1
  103.0 9.2 %grid_attention.3 = bf16[32,2,2,16,512]{4,3,2,1,0:T(8,128)(2,1)} custom-call(bf16[64,16,512]{2,1,0:T(8,128)(2,1)} %bitcast.20, bf16[512,1536]{1,0:T(8,128)(2,1)} %wqkv_ref.7, bf16[512,512]{1,0:T(8,128)(2,1)} %wo_ref.7, bf16[256,256]{1,0:T(8,128)(2,1)} %constant.9.clone.turn_ref, ...), custom_call_target="tpu_custom_call", output_to_operand_aliasing={{}: (5, {})} | custom-call | flops 2147483648 | bytes 4194304 | tf_op jit(solution)/shard_map/grid_attention/pallas_call | solution.py:117
  112.2 35.3 %all_to_all.15 = bf16[32,2,2,16,512]{4,3,2,1,0:T(8,128)(2,1)S(1)} all-to-all(bf16[32,2,2,16,512]{4,3,2,1,0:T(8,128)(2,1)} %grid_attention.3), channel_id=1, replica_groups={{0,4,8,12,16,20,24,28,32,36,40,44,48,52,56,60,64,68,72,76,80,84,88,92,9..., dimensions={0} | all-to-all | bytes 4194304 | tf_op jit(solution)/shard_map/all_to_all | solution.py:256
  147.5 1.5 %copy.22 = bf16[2,2,8,4,16,512]{5,4,3,2,1,0:T(8,128)(2,1)} copy(bf16[2,2,8,4,16,512]{5,4,0,1,3,2:T(8,128)(2,1)S(1)} %bitcast.17) | data formatting | bytes 4194304 | tf_op jit(solution)/shard_map/transpose | solution.py:282
  (4 shorter events, 0.0 us)
Async XLA Ops:
  0.9 5.6 %collective-permute-start.1 = (bf16[64,512]{1,0:T(8,128)(2,1)S(1)}, bf16[64,512]{1,0:T(8,128)(2,1)S(1)}, u32[]{:S(2)}, u32[]{:S(2)}) collective-permute-start(bf16[64,512]{1,0:T(8,128)(2,1)S(1)} %get-tuple-element.7), channel_id=1, source_target_pairs={{32,0},{64,32},{96,64},{33,1},{65,33},{97,65},{34,2},{66,34},{98,6... | collective-permute-start | bytes 196616 | tf_op jit(solution)/shard_map/ppermute | solution.py:264
  2.2 4.3 %collective-permute-start = (bf16[64,512]{1,0:T(8,128)(2,1)S(1)}, bf16[64,512]{1,0:T(8,128)(2,1)S(1)}, u32[]{:S(2)}, u32[]{:S(2)}) collective-permute-start(bf16[64,512]{1,0:T(8,128)(2,1)S(1)} %get-tuple-element.8), channel_id=1, source_target_pairs={{0,32},{32,64},{64,96},{1,33},{33,65},{65,97},{2,34},{34,66},{66,9... | collective-permute-start | bytes 196616 | tf_op jit(solution)/shard_map/ppermute | solution.py:263
  6.5 7.7 %copy-start.2 = (bf16[64,512]{1,0:T(8,128)(2,1)}, bf16[64,512]{1,0:T(8,128)(2,1)S(1)}, u32[]{:S(2)}) copy-start(bf16[64,512]{1,0:T(8,128)(2,1)S(1)} %collective-permute-done.1.bot_ref) | copy-start | bytes 196612
  6.5 7.7 %copy-start.3 = (bf16[64,512]{1,0:T(8,128)(2,1)}, bf16[64,512]{1,0:T(8,128)(2,1)S(1)}, u32[]{:S(2)}) copy-start(bf16[64,512]{1,0:T(8,128)(2,1)S(1)} %collective-permute-done.top_ref) | copy-start | bytes 196612
  6.6 6.0 %collective-permute-start.3 = (bf16[48,512]{1,0:T(8,128)(2,1)S(1)}, bf16[48,512]{1,0:T(8,128)(2,1)S(1)}, u32[]{:S(2)}, u32[]{:S(2)}) collective-permute-start(bf16[48,512]{1,0:T(8,128)(2,1)S(1)} %get-tuple-element.13), channel_id=1, source_target_pairs={{1,0},{2,1},{3,2},{4,3},{5,4},{6,5},{7,6},{8,7},{9,8},{10,9},{11,1... | collective-permute-start | bytes 147464 | tf_op jit(solution)/shard_map/ppermute | solution.py:271
  7.9 6.3 %collective-permute-start.2 = (bf16[48,512]{1,0:T(8,128)(2,1)S(1)}, bf16[48,512]{1,0:T(8,128)(2,1)S(1)}, u32[]{:S(2)}, u32[]{:S(2)}) collective-permute-start(bf16[48,512]{1,0:T(8,128)(2,1)S(1)} %get-tuple-element.14), channel_id=1, source_target_pairs={{0,1},{1,2},{2,3},{3,4},{4,5},{5,6},{6,7},{7,8},{8,9},{9,10},{10,1... | collective-permute-start | bytes 147464 | tf_op jit(solution)/shard_map/ppermute | solution.py:270
  12.6 1.6 %copy-start.4 = (bf16[48,512]{1,0:T(8,128)(2,1)}, bf16[48,512]{1,0:T(8,128)(2,1)S(1)}, u32[]{:S(2)}) copy-start(bf16[48,512]{1,0:T(8,128)(2,1)S(1)} %collective-permute-done.3.right_ref) | copy-start | bytes 147460
  14.2 0.6 copy-start.5
  34.1 38.8 %all-to-all-start.1 = ((bf16[32,2,16,512]{3,2,1,0:T(8,128)(2,1)}), bf16[32,2,16,512]{3,2,1,0:T(8,128)(2,1)S(1)}, u32[]{:S(2)}, u32[]{:S(2)}) async-start(bf16[32,2,16,512]{3,2,1,0:T(8,128)(2,1)} %bitcast.21), calls=%async_computation.1 | async-start | bytes 2097152 | tf_op jit(solution)/shard_map/all_to_all | solution.py:256
  72.9 9.4 %copy-start = (bf16[32,2,16,512]{3,2,1,0:T(8,128)(2,1)}, bf16[32,2,16,512]{3,2,1,0:T(8,128)(2,1)S(1)}, u32[]{:S(2)}) copy-start(bf16[32,2,16,512]{3,2,1,0:T(8,128)(2,1)S(1)} %all-to-all-done.1) | copy-start | bytes 3145732
  72.9 29.2 %all-to-all-start = ((bf16[32,2,16,512]{3,2,1,0:T(8,128)(2,1)}), bf16[32,2,16,512]{3,2,1,0:T(8,128)(2,1)S(1)}, u32[]{:S(2)}, u32[]{:S(2)}) async-start(bf16[32,2,16,512]{3,2,1,0:T(8,128)(2,1)} %bitcast.19), calls=%async_computation | async-start | bytes 2097152 | tf_op jit(solution)/shard_map/all_to_all | solution.py:256
  102.0 1.0 copy-start.1

commit v4 on v3

--- a/solution.py
+++ b/solution.py
@@ -84,11 +84,24 @@
         emit(half, x + mm(context[...], wo_ref[...]))
 
 
-def grid_kernel(x_ref, wqkv_ref, wo_ref, turn_ref, mask_ref, *rest):
-    out_ref, grouped, proj, context = rest[-4:]
+def weight_copies(wqkv_hbm, wo_hbm, wqkv_ref, wo_ref, sems):
+    return [
+        pltpu.make_async_copy(wqkv_hbm, wqkv_ref, sems.at[0]),
+        pltpu.make_async_copy(wo_hbm, wo_ref, sems.at[1]),
+    ]
+
+
+def grid_kernel(x_ref, turn_ref, mask_ref, wqkv_hbm, wo_hbm, *rest):
+    out_ref, grouped, proj, context, wqkv_ref, wo_ref, sems = rest[-7:]
+    copies = weight_copies(wqkv_hbm, wo_hbm, wqkv_ref, wo_ref, sems)
+    for copy in copies:
+        copy.start()
     for t in range(4):
         moved = mm(turn_ref[...], x_ref[16 * t : 16 * t + 16].reshape(256, CHANS))
         grouped[:, 16 * t : 16 * t + 16] = moved.astype(BF16).reshape(16, 16, CHANS)
+
+    for copy in copies:
+        copy.wait()
 
     def emit(half, rows):
         grouped[8 * half : 8 * half + 8] = rows.astype(BF16).reshape(8, 64, CHANS)
@@ -108,6 +121,9 @@
         pltpu.VMEM((16, 64, CHANS), BF16),
         pltpu.VMEM((512, 3 * CHANS), BF16),
         pltpu.VMEM((512, CHANS), BF16),
+        pltpu.VMEM((CHANS, 3 * CHANS), BF16),
+        pltpu.VMEM((CHANS, CHANS), BF16),
+        pltpu.SemaphoreType.DMA((2,)),
     ]
 
 
@@ -119,10 +135,10 @@
         grid=(1,),
         in_specs=[
             whole((64, 16, CHANS)),
-            whole((CHANS, 3 * CHANS)),
-            whole((CHANS, CHANS)),
             whole((256, 256)),
             whole((256, 128)),
+            pl.BlockSpec(memory_space=pl.ANY),
+            pl.BlockSpec(memory_space=pl.ANY),
             *[pl.BlockSpec(memory_space=pl.ANY) for _ in kept],
         ],
         out_specs=pl.BlockSpec((32, 1, 2, 16, CHANS), lambda s: (0, part, 0, 0, 0)),
@@ -134,39 +150,78 @@
             flops=8 * 1024 * CHANS * CHANS, bytes_accessed=4 * 2**20, transcendentals=2**20
         ),
         name="grid_attention",
-    )(x, qkv, out_proj, permutation((16, 16), (1, 0)), head_mask(), *kept)
+    )(x, permutation((16, 16), (1, 0)), head_mask(), qkv, out_proj, *kept)
+
+
+def expand_kernel(x_ref, w_ref, spread_ref, xp_ref, hid_ref, normed):
+    for pair in range(2):
+        moved = mm(spread_ref[...], x_ref[:, 2 * pair : 2 * pair + 2].reshape(256, CHANS))
+        xp_ref[2 * pair : 2 * pair + 2] = moved.astype(BF16).reshape(2, 8, 16, CHANS)
+        normed[256 * pair : 256 * pair + 256] = layer_norm(moved)
+    for at in range(0, WIDE, 256):
+        made = gelu(mm(normed[...], w_ref[:, at : at + 256])).astype(BF16)
+        hid_ref[:, :, :, at : at + 256] = made.reshape(4, 8, 16, 256)
+
+
+def expand(field, w_expand, after):
+    return pl.pallas_call(
+        lambda x, w, spread, _, *rest: expand_kernel(x, w, spread, *rest),
+        grid=(4,),
+        in_specs=[
+            pl.BlockSpec((2, 4, 64, CHANS), lambda s: (0, s, 0, 0)),
+            whole((CHANS, WIDE)),
+            whole((256, 256)),
+            pl.BlockSpec(memory_space=pl.ANY),
+        ],
+        out_specs=[
+            pl.BlockSpec((4, 8, 16, CHANS), lambda s: (s, 0, 0, 0)),
+            pl.BlockSpec((4, 8, 16, WIDE), lambda s: (s, 0, 0, 0)),
+        ],
+        out_shape=[
+            jax.ShapeDtypeStruct((16, 8, 16, CHANS), BF16),
+            jax.ShapeDtypeStruct((16, 8, 16, WIDE), BF16),
+        ],
+        scratch_shapes=[pltpu.VMEM((512, CHANS), BF16)],
+        compiler_params=params(),
+        cost_estimate=pl.CostEstimate(
+            flops=4 * 1024 * CHANS * WIDE, bytes_accessed=16 * 2**20, transcendentals=2048 * WIDE
+        ),
+        name="expand",
+    )(field.reshape(2, 16, 64, CHANS), w_expand, permutation((2, 2, 8, 8), (1, 3, 0, 2)), after)
 
 
 def local_kernel(
-    part, x_ref, prev_ref, next_ref, top_ref, bot_ref, left_ref, right_ref, we_ref, dw_ref, wp_ref, wqkv_ref, wo_ref,
-    spread_ref, turn_ref, mask_ref, out_ref, normed, pad, rim, spatial, acc, grouped, proj, context,
+    part, hid_ref, prev_ref, next_ref, xp_ref, rim_ref, left_ref, right_ref, we_ref, dw_ref, wp_ref,
+    spread_ref, turn_ref, mask_ref, wqkv_hbm, wo_hbm, out_ref, pad, normed, rim, spatial, acc, grouped, proj, context,
+    wqkv_ref, wo_ref, sems,
 ):
     step = pl.program_id(0)
+    copies = weight_copies(wqkv_hbm, wo_hbm, wqkv_ref, wo_ref, sems)
 
     @pl.when(step == 0)
     def _():
-        for pair in range(4):
-            moved = mm(spread_ref[...], x_ref[:, 2 * pair : 2 * pair + 2].reshape(256, CHANS))
-            acc[256 * pair : 256 * pair + 256] = moved
-            normed[128 + 256 * pair : 384 + 256 * pair] = layer_norm(moved)
+        for copy in copies:
+            copy.start()
+        normed[0:64] = mm(spread_ref[...], layer_norm(rim_ref[...].astype(F32))).astype(BF16)
+        normed[64:112] = layer_norm(left_ref[...].astype(F32))
+        normed[112:160] = layer_norm(right_ref[...].astype(F32))
+        acc[...] = xp_ref[...].reshape(1024, CHANS).astype(F32)
+
+    for at in range(0, CB, 256):
+        rim[:, at : at + 256] = gelu(mm(normed[...], we_ref[:, at : at + 256])).astype(BF16).astype(F32)
+    pad[1:9, 1:9] = hid_ref[...]
+    for j in range(8):
+        before = prev_ref[0, j]
+        after = next_ref[0, j]
         if part == 0:
-            before, after = (top_ref[...], prev_ref[0, 0]), (next_ref[0, 0], next_ref[1, 0])
+            before = jnp.concatenate([rim[8 * j : 8 * j + 8], before.astype(F32)[0:8]], axis=0).astype(BF16)
         else:
-            before, after = (prev_ref[0, 0], prev_ref[1, 0]), (next_ref[1, 0], bot_ref[...])
-        edges = jnp.concatenate([before[0], after[0], before[1], after[1]], axis=0)
-        moved = layer_norm(mm(spread_ref[...], edges))
-        normed[0:128] = moved[0:128]
-        normed[1152:1280] = moved[128:256]
-        normed[1280:1328] = layer_norm(left_ref[...].astype(F32))
-        normed[1328:1376] = layer_norm(right_ref[...].astype(F32))
-
-    for at in range(0, CB, 256):
-        hidden = gelu(mm(normed[...], we_ref[:, at : at + 256])).astype(BF16)
-        pad[:, 1:9, :, at : at + 256] = hidden[:1280].reshape(10, 8, 16, 256)
-        rim[:, at : at + 256] = hidden[1280:].astype(F32)
+            after = jnp.concatenate([after.astype(F32)[8:16], rim[8 * j : 8 * j + 8]], axis=0).astype(BF16)
+        pad[0, 1 + j] = before
+        pad[9, 1 + j] = after
     sub = lax.broadcasted_iota(jnp.int32, (8, CB), 0)
     for row in range(10):
-        at = 8 * part + row
+        at = 64 + 8 * part + row
         last = pad[row, 8].astype(F32)
         first = pad[row, 1].astype(F32)
         west, east = [], []
@@ -196,6 +251,8 @@
         for pair in range(4):
             mixed = acc[256 * pair : 256 * pair + 256].astype(BF16)
             grouped[:, 16 * pair : 16 * pair + 16] = mm(turn_ref[...], mixed).astype(BF16).reshape(16, 16, CHANS)
+        for copy in copies:
+            copy.wait()
 
         def emit(half, rows):
             rows = rows.reshape(4, 2, 8, 8, CHANS)
@@ -205,38 +262,38 @@
         attention(grouped, wqkv_ref, wo_ref, mask_ref, proj, context, emit)
 
 
-def local_part(part, field, rims, w_expand, dw_kernel, w_project, qkv, out_proj):
-    rows = field.reshape(2, 16, 64, CHANS)
+def local_part(part, xp, hid, rims, w_expand, dw_kernel, w_project, qkv, out_proj):
+    top, bottom, left, right = rims
 
     def edge(at):
-        return pl.BlockSpec((2, 1, 64, CHANS), lambda s: (0, at, 0, 0))
+        return pl.BlockSpec((1, 8, 16, CB), lambda s: (at, 0, 0, s))
 
     return pl.pallas_call(
         functools.partial(local_kernel, part),
         grid=(WIDE // CB,),
         in_specs=[
-            pl.BlockSpec((2, 8, 64, CHANS), lambda s: (0, part, 0, 0)),
+            pl.BlockSpec((8, 8, 16, CB), lambda s: (part, 0, 0, s)),
             edge((15, 7)[part]),
             edge((8, 0)[part]),
-            whole((64, CHANS)),
+            pl.BlockSpec((8, 8, 16, CHANS), lambda s: (part, 0, 0, 0)),
             whole((64, CHANS)),
             whole((48, CHANS)),
             whole((48, CHANS)),
             pl.BlockSpec((CHANS, CB), lambda s: (0, s)),
             pl.BlockSpec((3, 3, CB), lambda s: (0, 0, s)),
             pl.BlockSpec((CB, CHANS), lambda s: (s, 0)),
-            whole((CHANS, 3 * CHANS)),
-            whole((CHANS, CHANS)),
-            whole((256, 256)),
+            whole((64, 64)),
             whole((256, 256)),
             whole((256, 128)),
+            pl.BlockSpec(memory_space=pl.ANY),
+            pl.BlockSpec(memory_space=pl.ANY),
         ],
         out_specs=whole((8, 4, 2, 16, CHANS)),
         out_shape=jax.ShapeDtypeStruct((8, 4, 2, 16, CHANS), BF16),
         scratch_shapes=[
-            pltpu.VMEM((1376, CHANS), BF16),
             pltpu.VMEM((10, 10, 16, CB), BF16),
-            pltpu.VMEM((96, CB), F32),
+            pltpu.VMEM((160, CHANS), BF16),
+            pltpu.VMEM((160, CB), F32),
             pltpu.VMEM((8, 8, 16, CB), BF16),
             pltpu.VMEM((1024, CHANS), F32),
             *attention_scratch(),
@@ -247,8 +304,8 @@
         ),
         name="local_part",
     )(
-        rows, rows, rows, *rims, w_expand, dw_kernel, w_project, qkv, out_proj,
-        permutation((2, 2, 8, 8), (1, 3, 0, 2)), permutation((16, 16), (1, 0)), head_mask(),
+        hid, hid, hid, xp, (top, bottom)[part], left, right, w_expand, dw_kernel, w_project,
+        permutation((8, 8), (1, 0)), permutation((16, 16), (1, 0)), head_mask(), qkv, out_proj,
     )
 
 
@@ -267,13 +324,15 @@
     def rim(column):
         return jnp.concatenate([top[column : column + 1], field[:, column], bottom[column : column + 1], fill], axis=0)
 
-    left = lax.ppermute(rim(63), "col", [(i, i + 1) for i in range(n_col - 1)])
-    right = lax.ppermute(rim(0), "col", [(i + 1, i) for i in range(n_col - 1)])
+    east, west = rim(63), rim(0)
+    left = lax.ppermute(east, "col", [(i, i + 1) for i in range(n_col - 1)])
+    right = lax.ppermute(west, "col", [(i + 1, i) for i in range(n_col - 1)])
     rims = (top, bottom, left, right)
+    xp, hid = expand(field, w_expand, east)
     groups = [[32 * row + 4 * j + c for row in range(n_row) for j in range(8)] for c in range(4)]
     gathered = []
     for part in range(2):
-        blocked = local_part(part, field, rims, w_expand, dw_kernel, w_project, qkv_block, out_block)
+        blocked = local_part(part, xp, hid, rims, w_expand, dw_kernel, w_project, qkv_block, out_block)
         gathered.append(exchange(blocked.reshape(32, 2, 16, CHANS), groups).reshape(64, 16, CHANS))
     attended = None
     for part in range(2):

time: 150 us -> 151 us (level)
  starting transfers between devices: 38.5 us -> 26.4 us
  Pallas kernels: 56.9 us -> 63.8 us
  waiting for transfers between devices: 12.9 us -> 17.9 us
    pallas_call x0 -> x1, Pallas kernels: none -> 11 us  [expand(): pl.pallas_call(lambda x, w, spread, _, *rest: expand_kernel(x, w, spread,...]
    all_to_all x2, starting transfers between devices: 28.3 us -> 18 us  [exchange(): lax.all_to_all(blocks, ('row', 'col'), 0, 0, axis_index_groups=groups, ti...]
    pallas_call x2, Pallas kernels: 38.6 us -> 33.2 us  [local_part(): pl.pallas_call(functools.partial(local_kernel, part), grid=(WIDE // CB,),...]
    ppermute x1, waiting for transfers between devices: 0.01 us -> 4.77 us  [on_device(): bottom = lax.ppermute(field[0], 'row', up)]
    all_to_all x2, waiting for transfers between devices: 11.2 us -> 13.2 us  [exchange(): lax.all_to_all(blocks, ('row', 'col'), 0, 0, axis_index_groups=groups, ti...]
    ppermute x1, starting transfers between devices: 3.03 us -> 1.29 us  [on_device(): top = lax.ppermute(field[31], 'row', down)]
    ppermute x2, waiting for transfers between devices: 1.73 us -> 0.01 us  [the longest x1 0.01 us: on_device(): right = lax.ppermute(west, 'col', [(i + 1, i) for i in range(n_col - 1)])]
  transfers between devices with their start and end apart: 6 -> 6, of which waited for: 4 -> 3; matrix products, arithmetic and copies ran while one was open for 1% -> 1% of each run, Pallas kernels for 19% -> 25%
where the time goes in v4:
time: 151 us; the launch traced here: 149 us
  Pallas kernels  63.8 us (42%)
  blocking collectives  35.3 us (23%)
  starting transfers between devices  26.4 us (17%)
  waiting for transfers between devices  17.9 us (12%)
  local copies, waits for them, and re-layouts  5.26 us (3%)
    all_to_all x1, blocking collectives, exchange(): lax.all_to_all(blocks, ('row', 'col'), 0, 0, axis_index_groups=groups, ti...  35.3 us
    pallas_call x2, Pallas kernels, local_part(): pl.pallas_call(functools.partial(local_kernel, part), grid=(WIDE // CB,),...  33.2 us
    pallas_call x2, Pallas kernels, grid_attention(): pl.pallas_call(grid_kernel, grid=(1,), in_specs=[whole((64, 16, CHANS)),...  19.6 us
    all_to_all x2, starting transfers between devices, exchange(): lax.all_to_all(blocks, ('row', 'col'), 0, 0, axis_index_groups=groups, ti...  18 us
    all_to_all x2, waiting for transfers between devices, exchange(): lax.all_to_all(blocks, ('row', 'col'), 0, 0, axis_index_groups=groups, ti...  13.2 us
    pallas_call x1, Pallas kernels, expand(): pl.pallas_call(lambda x, w, spread, _, *rest: expand_kernel(x, w, spread,...  11 us
    ppermute x1, waiting for transfers between devices, on_device(): bottom = lax.ppermute(field[0], 'row', up)  4.77 us
    ppermute x1, starting transfers between devices, on_device(): left = lax.ppermute(east, 'col', [(i, i + 1) for i in range(n_col - 1)])  4.55 us
  transfers between devices with their start and end apart: 6, of which 3 were waited for; matrix products, arithmetic and copies ran while one was open for 1% of the time, Pallas kernels for 25%

profile of v4, /device:TPU:0, one launch (start us, length us, event | category | flops | bytes accessed | tf_op | source)
XLA Modules:
  0.0 148.9 jit_solution(1072978805615814367)
XLA Ops:
  0.0 0.9 slice_bitcast_fusion.1
  0.9 1.3 collective-permute-start
  2.2 1.3 collective-permute-start.1
  3.5 1.1 fusion
  4.7 0.1 pad.7.clone
  4.7 0.0 collective-permute-done.rim_ref
  4.7 0.0 copy-start.5
  4.8 4.8 %collective-permute-done.1.rim_ref = bf16[64,512]{1,0:T(8,128)(2,1)S(1)} collective-permute-done((bf16[64,512]{1,0:T(8,128)(2,1)S(1)}, bf16[64,512]{1,0:T(8,128)(2,1)S(1)}, u32[]{:S(2)}, u32[]{:S(2)}) %collective-permute-start.1) | collective-permute-done | bytes 65568 | tf_op jit(solution)/shard_map/ppermute | solution.py:321
  9.5 0.0 copy-start.4
  9.5 0.1 maximum_maximum_fusion.1
  9.6 0.0 copy-start.6
  9.6 1.3 collective-permute-start.3
  10.9 4.5 %collective-permute-start.2 = (bf16[48,512]{1,0:T(8,128)(2,1)S(1)}, bf16[48,512]{1,0:T(8,128)(2,1)S(1)}, u32[]{:S(2)}, u32[]{:S(2)}) collective-permute-start(bf16[48,512]{1,0:T(8,128)(2,1)S(1)} %get-tuple-element.18._), channel_id=1, source_target_pairs={{0,1},{1,2},{2,3},{3,4},{4,5},{5,6},{6,7},{7,8},{8,9},{9,10},{10,1... | collective-permute-start | bytes 147464 | tf_op jit(solution)/shard_map/ppermute | solution.py:328
  15.5 0.0 copy-done.6
  15.5 11.0 %expand.1 = (bf16[16,8,16,512]{3,2,1,0:T(8,128)(2,1)}, bf16[16,8,16,2048]{3,2,1,0:T(8,128)(2,1)}) custom-call(bf16[2,16,64,512]{3,2,1,0:T(8,128)(2,1)} %bitcast.22, bf16[512,2048]{1,0:T(8,128)(2,1)} %we_ref.3, bf16[256,256]{1,0:T(8,128)(2,1)} %constant.10.clone.spread, bf16[48,512]{1,0:T(8,128)(2,1)} %copy-done.6), custom_call_target="tpu_custom_call" | custom-call | flops 4294967296 | bytes 16777216 | tf_op jit(solution)/shard_map/expand/pallas_call | solution.py:167
  26.5 0.0 copy-done.5
  26.5 0.0 copy-done.4
  26.5 0.0 collective-permute-done.3.right_ref
  26.5 0.0 copy-start.2
  26.5 0.0 collective-permute-done.2.left_ref
  26.5 0.0 copy-start.3
  26.5 0.6 copy-done.2
  27.1 0.0 copy-done.3
  27.1 16.6 %local_part.3 = bf16[8,4,2,16,512]{4,3,2,1,0:T(8,128)(2,1)} custom-call(bf16[16,8,16,2048]{3,2,1,0:T(8,128)(2,1)} %get-tuple-element.7.hid_ref.prev_ref.next_ref, bf16[16,8,16,2048]{3,2,1,0:T(8,128)(2,1)} %get-tuple-element.7.hid_ref.prev_ref.next_ref, bf16[16,8,16,2048]{3,2,1,0:T(8,128)(2,1)} %get-tuple-element.7.hid_ref.prev_ref.next_ref, ...), custom_call_target="tpu_custom_call" | custom-call | flops 4294967296 | bytes 8388608 | tf_op jit(solution)/shard_map/local_part/pallas_call | solution.py:271
  43.7 11.3 %all-to-all-start.1 = ((bf16[32,2,16,512]{3,2,1,0:T(8,128)(2,1)}), bf16[32,2,16,512]{3,2,1,0:T(8,128)(2,1)S(1)}, u32[]{:S(2)}, u32[]{:S(2)}) async-start(bf16[32,2,16,512]{3,2,1,0:T(8,128)(2,1)} %bitcast.19), calls=%async_computation.1 | async-start | bytes 2097152 | tf_op jit(solution)/shard_map/all_to_all | solution.py:313
  55.0 16.7 %local_part.2 = bf16[8,4,2,16,512]{4,3,2,1,0:T(8,128)(2,1)} custom-call(bf16[16,8,16,2048]{3,2,1,0:T(8,128)(2,1)} %get-tuple-element.7.hid_ref.prev_ref.next_ref, bf16[16,8,16,2048]{3,2,1,0:T(8,128)(2,1)} %get-tuple-element.7.hid_ref.prev_ref.next_ref, bf16[16,8,16,2048]{3,2,1,0:T(8,128)(2,1)} %get-tuple-element.7.hid_ref.prev_ref.next_ref, ...), custom_call_target="tpu_custom_call" | custom-call | flops 4294967296 | bytes 8388608 | tf_op jit(solution)/shard_map/local_part/pallas_call | solution.py:271
  71.6 3.2 %all-to-all-done.1 = bf16[32,2,16,512]{3,2,1,0:T(8,128)(2,1)S(1)} async-done(((bf16[32,2,16,512]{3,2,1,0:T(8,128)(2,1)}), bf16[32,2,16,512]{3,2,1,0:T(8,128)(2,1)S(1)}, u32[]{:S(2)}, u32[]{:S(2)}) %all-to-all-start.1) | async-done | bytes 1048608 | tf_op jit(solution)/shard_map/all_to_all | solution.py:313
  74.8 0.0 copy-start
  74.8 6.7 %all-to-all-start = ((bf16[32,2,16,512]{3,2,1,0:T(8,128)(2,1)}), bf16[32,2,16,512]{3,2,1,0:T(8,128)(2,1)S(1)}, u32[]{:S(2)}, u32[]{:S(2)}) async-start(bf16[32,2,16,512]{3,2,1,0:T(8,128)(2,1)} %bitcast.18), calls=%async_computation | async-start | bytes 2097152 | tf_op jit(solution)/shard_map/all_to_all | solution.py:313
  81.5 0.0 copy-done
  81.5 9.8 %grid_attention.2.rest_0_ = bf16[32,2,2,16,512]{4,3,2,1,0:T(8,128)(2,1)} custom-call(bf16[64,16,512]{2,1,0:T(8,128)(2,1)} %bitcast.20, bf16[256,256]{1,0:T(8,128)(2,1)} %constant.12.clone.turn_ref, bf16[256,128]{1,0:T(8,128)(2,1)} %constant.13.clone.mask_ref, bf16[512,1536]{1,0:T(8,128)(2,1)} %wqkv_hbm.7, bf16[512,512]{1,0:T(8,128)(2,1)} %wo_hbm.7), custom_call_target="tpu_custom_call" | custom-call | flops 2147483648 | bytes 4194304 | tf_op jit(solution)/shard_map/grid_attention/pallas_call | solution.py:133
  91.3 10.0 %all-to-all-done = bf16[32,2,16,512]{3,2,1,0:T(8,128)(2,1)S(1)} async-done(((bf16[32,2,16,512]{3,2,1,0:T(8,128)(2,1)}), bf16[32,2,16,512]{3,2,1,0:T(8,128)(2,1)S(1)}, u32[]{:S(2)}, u32[]{:S(2)}) %all-to-all-start) | async-done | bytes 1048608 | tf_op jit(solution)/shard_map/all_to_all | solution.py:313
  101.3 0.0 copy-start.1
  101.3 1.0 copy-done.1
  102.3 9.8 %grid_attention.3 = bf16[32,2,2,16,512]{4,3,2,1,0:T(8,128)(2,1)} custom-call(bf16[64,16,512]{2,1,0:T(8,128)(2,1)} %bitcast.21, bf16[256,256]{1,0:T(8,128)(2,1)} %constant.12.clone.turn_ref, bf16[256,128]{1,0:T(8,128)(2,1)} %constant.13.clone.mask_ref, bf16[512,1536]{1,0:T(8,128)(2,1)} %wqkv_hbm.7, ...), custom_call_target="tpu_custom_call", output_to_operand_aliasing={{}: (5, {})} | custom-call | flops 2147483648 | bytes 4194304 | tf_op jit(solution)/shard_map/grid_attention/pallas_call | solution.py:133
  112.1 35.3 %all_to_all.15 = bf16[32,2,2,16,512]{4,3,2,1,0:T(8,128)(2,1)S(1)} all-to-all(bf16[32,2,2,16,512]{4,3,2,1,0:T(8,128)(2,1)} %grid_attention.3), channel_id=1, replica_groups={{0,4,8,12,16,20,24,28,32,36,40,44,48,52,56,60,64,68,72,76,80,84,88,92,9..., dimensions={0} | all-to-all | bytes 4194304 | tf_op jit(solution)/shard_map/all_to_all | solution.py:313
  147.4 1.5 %copy.23 = bf16[2,2,8,4,16,512]{5,4,3,2,1,0:T(8,128)(2,1)} copy(bf16[2,2,8,4,16,512]{5,4,0,1,3,2:T(8,128)(2,1)S(1)} %bitcast.17) | data formatting | bytes 4194304 | tf_op jit(solution)/shard_map/transpose | solution.py:341
  (4 shorter events, 0.0 us)
Async XLA Ops:
  0.9 3.9 %collective-permute-start = (bf16[64,512]{1,0:T(8,128)(2,1)S(1)}, bf16[64,512]{1,0:T(8,128)(2,1)S(1)}, u32[]{:S(2)}, u32[]{:S(2)}) collective-permute-start(bf16[64,512]{1,0:T(8,128)(2,1)S(1)} %get-tuple-element.11), channel_id=1, source_target_pairs={{0,32},{32,64},{64,96},{1,33},{33,65},{65,97},{2,34},{34,66},{66,9... | collective-permute-start | bytes 196616 | tf_op jit(solution)/shard_map/ppermute | solution.py:320
  2.2 7.3 %collective-permute-start.1 = (bf16[64,512]{1,0:T(8,128)(2,1)S(1)}, bf16[64,512]{1,0:T(8,128)(2,1)S(1)}, u32[]{:S(2)}, u32[]{:S(2)}) collective-permute-start(bf16[64,512]{1,0:T(8,128)(2,1)S(1)} %get-tuple-element.12), channel_id=1, source_target_pairs={{32,0},{64,32},{96,64},{33,1},{65,33},{97,65},{34,2},{66,34},{98,6... | collective-permute-start | bytes 196616 | tf_op jit(solution)/shard_map/ppermute | solution.py:321
  4.7 21.7 %copy-start.5 = (bf16[64,512]{1,0:T(8,128)(2,1)}, bf16[64,512]{1,0:T(8,128)(2,1)S(1)}, u32[]{:S(2)}) copy-start(bf16[64,512]{1,0:T(8,128)(2,1)S(1)} %collective-permute-done.rim_ref) | copy-start | bytes 196612
  9.5 16.9 %copy-start.4 = (bf16[64,512]{1,0:T(8,128)(2,1)}, bf16[64,512]{1,0:T(8,128)(2,1)S(1)}, u32[]{:S(2)}) copy-start(bf16[64,512]{1,0:T(8,128)(2,1)S(1)} %collective-permute-done.1.rim_ref) | copy-start | bytes 196612
  9.6 5.9 %copy-start.6 = (bf16[48,512]{1,0:T(8,128)(2,1)}, bf16[48,512]{1,0:T(8,128)(2,1)S(1)}, u32[]{:S(2)}) copy-start(bf16[48,512]{1,0:T(8,128)(2,1)S(1)} %get-tuple-element.18._) | copy-start | bytes 147460
  9.6 16.8 %collective-permute-start.3 = (bf16[48,512]{1,0:T(8,128)(2,1)S(1)}, bf16[48,512]{1,0:T(8,128)(2,1)S(1)}, u32[]{:S(2)}, u32[]{:S(2)}) collective-permute-start(bf16[48,512]{1,0:T(8,128)(2,1)S(1)} %get-tuple-element.17), channel_id=1, source_target_pairs={{1,0},{2,1},{3,2},{4,3},{5,4},{6,5},{7,6},{8,7},{9,8},{10,9},{11,1... | collective-permute-start | bytes 147464 | tf_op jit(solution)/shard_map/ppermute | solution.py:329
  10.9 15.6 %collective-permute-start.2 = (bf16[48,512]{1,0:T(8,128)(2,1)S(1)}, bf16[48,512]{1,0:T(8,128)(2,1)S(1)}, u32[]{:S(2)}, u32[]{:S(2)}) collective-permute-start(bf16[48,512]{1,0:T(8,128)(2,1)S(1)} %get-tuple-element.18._), channel_id=1, source_target_pairs={{0,1},{1,2},{2,3},{3,4},{4,5},{5,6},{6,7},{7,8},{8,9},{9,10},{10,1... | collective-permute-start | bytes 147464 | tf_op jit(solution)/shard_map/ppermute | solution.py:328
  26.5 0.6 copy-start.2
  26.5 0.6 copy-start.3
  43.7 31.1 %all-to-all-start.1 = ((bf16[32,2,16,512]{3,2,1,0:T(8,128)(2,1)}), bf16[32,2,16,512]{3,2,1,0:T(8,128)(2,1)S(1)}, u32[]{:S(2)}, u32[]{:S(2)}) async-start(bf16[32,2,16,512]{3,2,1,0:T(8,128)(2,1)} %bitcast.19), calls=%async_computation.1 | async-start | bytes 2097152 | tf_op jit(solution)/shard_map/all_to_all | solution.py:313
  74.8 6.7 %copy-start = (bf16[32,2,16,512]{3,2,1,0:T(8,128)(2,1)}, bf16[32,2,16,512]{3,2,1,0:T(8,128)(2,1)S(1)}, u32[]{:S(2)}) copy-start(bf16[32,2,16,512]{3,2,1,0:T(8,128)(2,1)S(1)} %all-to-all-done.1) | copy-start | bytes 3145732
  74.8 26.5 %all-to-all-start = ((bf16[32,2,16,512]{3,2,1,0:T(8,128)(2,1)}), bf16[32,2,16,512]{3,2,1,0:T(8,128)(2,1)S(1)}, u32[]{:S(2)}, u32[]{:S(2)}) async-start(bf16[32,2,16,512]{3,2,1,0:T(8,128)(2,1)} %bitcast.18), calls=%async_computation | async-start | bytes 2097152 | tf_op jit(solution)/shard_map/all_to_all | solution.py:313
  101.3 1.0 copy-start.1

commit v5 on v3

--- a/solution.py
+++ b/solution.py
@@ -14,7 +14,7 @@
 CHANS = 512
 WIDE = 2048
 CB = 1024
-VMEM_LIMIT = 56 * 2**20
+VMEM_LIMIT = 24 * 2**20
 SCALE_LOG2 = float(HEAD**-0.5 * np.log2(np.e))
 
 

time: 150 us -> 162 us (1.080)
  local copies, waits for them, and re-layouts: 5.24 us -> 26.7 us
  Pallas kernels: 56.9 us -> 47.4 us
    unnamed x12 -> x46, local copies, waits for them, and re-layouts: 1.6 us -> 23.1 us
    pallas_call x2, Pallas kernels: 38.6 us -> 33.5 us  [local_part(): pl.pallas_call(functools.partial(local_kernel, part), grid=(WIDE // CB,),...]
    pallas_call x2, Pallas kernels: 18.3 us -> 13.9 us  [grid_attention(): pl.pallas_call(grid_kernel, grid=(1,), in_specs=[whole((64, 16, CHANS)),...]
  transfers between devices with their start and end apart: 6 -> 6, of which waited for: 4 -> 3; matrix products, arithmetic and copies ran while one was open for 1% -> 1% of each run, Pallas kernels for 19% -> 14%
where the time goes in v5:
time: 162 us; the launch traced here: 161 us
  Pallas kernels  47.4 us (29%)
  starting transfers between devices  39.4 us (24%)
  blocking collectives  34.3 us (21%)
  local copies, waits for them, and re-layouts  26.7 us (16%)
  waiting for transfers between devices  12.7 us (8%)
    all_to_all x1, blocking collectives, exchange(): lax.all_to_all(blocks, ('row', 'col'), 0, 0, axis_index_groups=groups, ti...  34.3 us
    pallas_call x2, Pallas kernels, local_part(): pl.pallas_call(functools.partial(local_kernel, part), grid=(WIDE // CB,),...  33.5 us
    all_to_all x2, starting transfers between devices, exchange(): lax.all_to_all(blocks, ('row', 'col'), 0, 0, axis_index_groups=groups, ti...  29.2 us
    unnamed x46, local copies, waits for them, and re-layouts  23.1 us
    pallas_call x2, Pallas kernels, grid_attention(): pl.pallas_call(grid_kernel, grid=(1,), in_specs=[whole((64, 16, CHANS)),...  13.9 us
    all_to_all x2, waiting for transfers between devices, exchange(): lax.all_to_all(blocks, ('row', 'col'), 0, 0, axis_index_groups=groups, ti...  11 us
    ppermute x1, starting transfers between devices, on_device(): left = lax.ppermute(rim(63), 'col', [(i, i + 1) for i in range(n_col - 1)])  4.55 us
  transfers between devices with their start and end apart: 6, of which 3 were waited for; matrix products, arithmetic and copies ran while one was open for 1% of the time, Pallas kernels for 14%

profile of v5, /device:TPU:0, one launch (start us, length us, event | category | flops | bytes accessed | tf_op | source)
XLA Modules:
  0.0 160.8 jit_solution(12038341250959011778)
XLA Ops:
  0.0 0.9 slice_bitcast_fusion
  0.9 1.3 collective-permute-start.1
  2.2 3.0 %collective-permute-start = (bf16[64,512]{1,0:T(8,128)(2,1)S(1)}, bf16[64,512]{1,0:T(8,128)(2,1)S(1)}, u32[]{:S(2)}, u32[]{:S(2)}) collective-permute-start(bf16[64,512]{1,0:T(8,128)(2,1)S(1)} %get-tuple-element.8), channel_id=1, source_target_pairs={{0,32},{32,64},{64,96},{1,33},{33,65},{65,97},{2,34},{34,66},{66,9... | collective-permute-start | bytes 196616 | tf_op jit(solution)/shard_map/ppermute | solution.py:263
  5.2 1.1 fusion
  6.4 0.1 pad.7.clone
  6.5 0.0 collective-permute-done.1.bot_ref
  6.5 0.0 collective-permute-done.top_ref
  6.5 0.1 maximum_maximum_fusion.1
  6.6 1.3 collective-permute-start.3
  7.9 4.5 %collective-permute-start.2 = (bf16[48,512]{1,0:T(8,128)(2,1)S(1)}, bf16[48,512]{1,0:T(8,128)(2,1)S(1)}, u32[]{:S(2)}, u32[]{:S(2)}) collective-permute-start(bf16[48,512]{1,0:T(8,128)(2,1)S(1)} %get-tuple-element.14), channel_id=1, source_target_pairs={{0,1},{1,2},{2,3},{3,4},{4,5},{5,6},{6,7},{7,8},{8,9},{9,10},{10,1... | collective-permute-start | bytes 147464 | tf_op jit(solution)/shard_map/ppermute | solution.py:270
  12.5 0.1 collective-permute-done.3.right_ref
  12.6 1.6 collective-permute-done.2.left_ref
  14.2 0.0 copy-start
  14.2 1.6 copy-done
  15.8 1.6 copy-done.2
  17.4 1.6 copy-done.4
  19.0 1.4 copy-done.6
  20.4 1.0 copy-done.10
  21.4 0.9 copy-done.14
  22.3 0.9 copy-done.16
  23.2 0.9 copy-done.19
  24.1 0.8 copy-done.21
  25.0 16.8 %local_part.3 = bf16[8,4,2,16,512]{4,3,2,1,0:T(8,128)(2,1)} custom-call(bf16[2,16,64,512]{3,2,1,0:T(8,128)(2,1)S(1)} %bitcast.18, bf16[2,16,64,512]{3,2,1,0:T(8,128)(2,1)S(1)} %bitcast.19, bf16[2,16,64,512]{3,2,1,0:T(8,128)(2,1)S(1)} %bitcast.20, bf16[64,512]{1,0:T(8,128)(2,1)S(1)} %collective-permute-done.top_ref, ...), custom_call_target="tpu_custom_call" | custom-call | flops 4294967296 | bytes 8388608 | tf_op jit(solution)/shard_map/local_part/pallas_call | solution.py:214
  41.7 19.1 %all-to-all-start.1 = ((bf16[32,2,16,512]{3,2,1,0:T(8,128)(2,1)}), bf16[32,2,16,512]{3,2,1,0:T(8,128)(2,1)S(1)}, u32[]{:S(2)}, u32[]{:S(2)}) async-start(bf16[32,2,16,512]{3,2,1,0:T(8,128)(2,1)} %bitcast.7), calls=%async_computation.1 | async-start | bytes 2097152 | tf_op jit(solution)/shard_map/all_to_all | solution.py:256
  60.8 0.0 copy-done.15
  60.8 0.0 copy-done.22
  60.9 0.0 copy-done.1
  60.9 0.0 copy-start.3
  60.9 1.6 copy-done.3
  62.5 1.6 copy-done.5
  64.1 1.4 copy-done.7
  65.5 1.0 copy-done.11
  66.5 0.9 copy-done.17
  67.4 0.9 copy-done.20
  68.3 16.8 %local_part.2 = bf16[8,4,2,16,512]{4,3,2,1,0:T(8,128)(2,1)} custom-call(bf16[2,16,64,512]{3,2,1,0:T(8,128)(2,1)S(1)} %bitcast.21, bf16[2,16,64,512]{3,2,1,0:T(8,128)(2,1)S(1)} %bitcast.22, bf16[2,16,64,512]{3,2,1,0:T(8,128)(2,1)S(1)} %bitcast.23, bf16[64,512]{1,0:T(8,128)(2,1)S(1)} %collective-permute-done.top_ref, ...), custom_call_target="tpu_custom_call" | custom-call | flops 4294967296 | bytes 8388608 | tf_op jit(solution)/shard_map/local_part/pallas_call | solution.py:214
  85.1 0.0 all-to-all-done.1
  85.1 10.1 %all-to-all-start = ((bf16[32,2,16,512]{3,2,1,0:T(8,128)(2,1)}), bf16[32,2,16,512]{3,2,1,0:T(8,128)(2,1)}, u32[]{:S(2)}, u32[]{:S(2)}) async-start(bf16[32,2,16,512]{3,2,1,0:T(8,128)(2,1)} %bitcast.5), calls=%async_computation | async-start | bytes 2097152 | tf_op jit(solution)/shard_map/all_to_all | solution.py:256
  95.2 0.0 copy-done.18
  95.2 0.0 copy-start.8
  95.2 1.4 copy-done.8
  96.6 1.0 copy-done.12
  97.7 6.3 %grid_attention.2.rest_0_ = bf16[32,2,2,16,512]{4,3,2,1,0:T(8,128)(2,1)S(1)} custom-call(bf16[64,16,512]{2,1,0:T(8,128)(2,1)S(1)} %bitcast.17, bf16[512,1536]{1,0:T(8,128)(2,1)S(1)} %copy-done.8, bf16[512,512]{1,0:T(8,128)(2,1)S(1)} %copy-done.12, bf16[256,256]{1,0:T(8,128)(2,1)S(1)} %copy-done.18, bf16[256,128]{1,0:T(8,128)(2,1)S(1)} %copy-done.22), custom_call_target="tpu_custom_call" | custom-call | flops 2147483648 | bytes 4194304 | tf_op jit(solution)/shard_map/grid_attention/pallas_call | solution.py:117
  104.0 11.0 %all-to-all-done = bf16[32,2,16,512]{3,2,1,0:T(8,128)(2,1)} async-done(((bf16[32,2,16,512]{3,2,1,0:T(8,128)(2,1)}), bf16[32,2,16,512]{3,2,1,0:T(8,128)(2,1)}, u32[]{:S(2)}, u32[]{:S(2)}) %all-to-all-start) | async-done | bytes 1048608 | tf_op jit(solution)/shard_map/all_to_all | solution.py:256
  115.0 1.4 copy-done.9
  116.4 1.0 copy-done.13
  117.4 7.6 %grid_attention.3 = bf16[32,2,2,16,512]{4,3,2,1,0:T(8,128)(2,1)S(1)} custom-call(bf16[64,16,512]{2,1,0:T(8,128)(2,1)} %bitcast.6.x_ref, bf16[512,1536]{1,0:T(8,128)(2,1)S(1)} %copy-done.9, bf16[512,512]{1,0:T(8,128)(2,1)S(1)} %copy-done.13, bf16[256,256]{1,0:T(8,128)(2,1)S(1)} %copy-done.18, ...), custom_call_target="tpu_custom_call", output_to_operand_aliasing={{}: (5, {})} | custom-call | flops 2147483648 | bytes 4194304 | tf_op jit(solution)/shard_map/grid_attention/pallas_call | solution.py:117
  125.0 34.3 %all_to_all.15 = bf16[32,2,2,16,512]{4,3,2,1,0:T(8,128)(2,1)S(1)} all-to-all(bf16[32,2,2,16,512]{4,3,2,1,0:T(8,128)(2,1)S(1)} %grid_attention.3), channel_id=1, replica_groups={{0,4,8,12,16,20,24,28,32,36,40,44,48,52,56,60,64,68,72,76,80,84,88,92,9..., dimensions={0} | all-to-all | bytes 4194304 | tf_op jit(solution)/shard_map/all_to_all | solution.py:256
  159.3 1.5 copy.22
  (24 shorter events, 0.1 us)
Async XLA Ops:
  0.9 5.6 %collective-permute-start.1 = (bf16[64,512]{1,0:T(8,128)(2,1)S(1)}, bf16[64,512]{1,0:T(8,128)(2,1)S(1)}, u32[]{:S(2)}, u32[]{:S(2)}) collective-permute-start(bf16[64,512]{1,0:T(8,128)(2,1)S(1)} %get-tuple-element.7), channel_id=1, source_target_pairs={{32,0},{64,32},{96,64},{33,1},{65,33},{97,65},{34,2},{66,34},{98,6... | collective-permute-start | bytes 196616 | tf_op jit(solution)/shard_map/ppermute | solution.py:264
  2.2 4.3 %collective-permute-start = (bf16[64,512]{1,0:T(8,128)(2,1)S(1)}, bf16[64,512]{1,0:T(8,128)(2,1)S(1)}, u32[]{:S(2)}, u32[]{:S(2)}) collective-permute-start(bf16[64,512]{1,0:T(8,128)(2,1)S(1)} %get-tuple-element.8), channel_id=1, source_target_pairs={{0,32},{32,64},{64,96},{1,33},{33,65},{65,97},{2,34},{34,66},{66,9... | collective-permute-start | bytes 196616 | tf_op jit(solution)/shard_map/ppermute | solution.py:263
  6.6 6.0 %collective-permute-start.3 = (bf16[48,512]{1,0:T(8,128)(2,1)S(1)}, bf16[48,512]{1,0:T(8,128)(2,1)S(1)}, u32[]{:S(2)}, u32[]{:S(2)}) collective-permute-start(bf16[48,512]{1,0:T(8,128)(2,1)S(1)} %get-tuple-element.13), channel_id=1, source_target_pairs={{1,0},{2,1},{3,2},{4,3},{5,4},{6,5},{7,6},{8,7},{9,8},{10,9},{11,1... | collective-permute-start | bytes 147464 | tf_op jit(solution)/shard_map/ppermute | solution.py:271
  7.9 6.3 %collective-permute-start.2 = (bf16[48,512]{1,0:T(8,128)(2,1)S(1)}, bf16[48,512]{1,0:T(8,128)(2,1)S(1)}, u32[]{:S(2)}, u32[]{:S(2)}) collective-permute-start(bf16[48,512]{1,0:T(8,128)(2,1)S(1)} %get-tuple-element.14), channel_id=1, source_target_pairs={{0,1},{1,2},{2,3},{3,4},{4,5},{5,6},{6,7},{7,8},{8,9},{9,10},{10,1... | collective-permute-start | bytes 147464 | tf_op jit(solution)/shard_map/ppermute | solution.py:270
  14.2 1.6 copy-start
  15.8 1.6 copy-start.2
  17.4 1.6 copy-start.4
  19.0 1.4 copy-start.6
  20.4 1.0 copy-start.10
  21.4 0.9 copy-start.14
  22.3 0.9 copy-start.16
  23.2 0.9 copy-start.19
  24.1 0.8 copy-start.21
  25.0 35.9 %copy-start.15 = (f32[3,3,2048]{2,1,0:T(4,128)S(1)}, f32[3,3,2048]{2,1,0:T(4,128)}, u32[]{:S(2)}) copy-start(f32[3,3,2048]{2,1,0:T(4,128)} %dw_ref.3) | copy-start | bytes 221188
  25.0 35.9 %copy-start.22 = (bf16[256,128]{1,0:T(8,128)(2,1)S(1)}, bf16[256,128]{1,0:T(8,128)(2,1)}, u32[]{:S(2)}) copy-start(bf16[256,128]{1,0:T(8,128)(2,1)} %constant.10.clone.mask_ref) | copy-start | bytes 196612
  41.7 19.1 %copy-start.1 = (bf16[32,64,512]{2,1,0:T(8,128)(2,1)S(1)}, bf16[32,64,512]{2,1,0:T(8,128)(2,1)}, u32[]{:S(2)}) copy-start(bf16[32,64,512]{2,1,0:T(8,128)(2,1)} %param.18) | copy-start | bytes 6291460
  41.7 43.4 %all-to-all-start.1 = ((bf16[32,2,16,512]{3,2,1,0:T(8,128)(2,1)}), bf16[32,2,16,512]{3,2,1,0:T(8,128)(2,1)S(1)}, u32[]{:S(2)}, u32[]{:S(2)}) async-start(bf16[32,2,16,512]{3,2,1,0:T(8,128)(2,1)} %bitcast.7), calls=%async_computation.1 | async-start | bytes 2097152 | tf_op jit(solution)/shard_map/all_to_all | solution.py:256
  60.9 1.6 copy-start.3
  62.5 1.6 copy-start.5
  64.1 1.4 copy-start.7
  65.5 1.0 copy-start.11
  66.5 0.9 copy-start.17
  67.4 0.9 copy-start.20
  85.1 10.1 %copy-start.18 = (bf16[256,256]{1,0:T(8,128)(2,1)S(1)}, bf16[256,256]{1,0:T(8,128)(2,1)}, u32[]{:S(2)}) copy-start(bf16[256,256]{1,0:T(8,128)(2,1)} %constant.9.clone.turn_ref) | copy-start | bytes 393220
  85.1 29.9 %all-to-all-start = ((bf16[32,2,16,512]{3,2,1,0:T(8,128)(2,1)}), bf16[32,2,16,512]{3,2,1,0:T(8,128)(2,1)}, u32[]{:S(2)}, u32[]{:S(2)}) async-start(bf16[32,2,16,512]{3,2,1,0:T(8,128)(2,1)} %bitcast.5), calls=%async_computation | async-start | bytes 2097152 | tf_op jit(solution)/shard_map/all_to_all | solution.py:256
  95.2 1.4 copy-start.8
  96.6 1.0 copy-start.12
  115.0 1.4 copy-start.9
  116.4 1.0 copy-start.13
